TPU v7x, 128 devices: a whole 4x4x4 slice. The times are simulated.
128 devices in a mesh: grp: 8 (over x, core), dev: 16 (over z, y).
Axes of the slice: x: 4, y: 4, z: 4, core: 2. Of those that a mesh axis runs over, the one named last changes fastest.
Arguments:
- points: bfloat16 [65536, 1024], P(('grp', 'dev')), may hold values from -100 to 100
- coarse: int32 [65536, 1], P(('grp', 'dev')), may hold values from 0 to 31; in each aligned block of 512 rows (0 to 511, 512 to 1023, ...) at most 32 rows name the same one
- candidates: int32 [32, 4], replicated, may hold values from 0 to 7, as said below
- centroids: bfloat16 [8192, 1024], P(('grp', 'dev')), may hold values from -0.1875 to 0.1875
Outputs:
- new_centroids: float32 [8192, 1024], P(('grp', 'dev'))
- point_affinity: float32 [65536], P(('grp', 'dev'))
Inputs may be any that keep to these rules, and one draw needn't show every extreme that they name: In the rows of one device no coarse cluster is named by more than 32 rows. `candidates`: each row lists 4 different blocks.
All inputs are finite; a program needn't handle non-finite values.
Results may differ from a plain program's by a relative error of at most 0.0045.
Values may be sent and summed in bfloat16 or wider, within the bound.
A program may use at most 64 MiB of HBM per device.

v0:
```python
import jax
import jax.numpy as jnp
from jax import lax
from jax.sharding import PartitionSpec as P

BLK = 128


SOFTMAX_TEMP = 0.4
PRIOR_WEIGHT = 1.0


def softmax_parts(logit_scores):
    top_logit = jnp.max(logit_scores, axis=1, keepdims=True)
    exponent_values = jnp.exp(logit_scores - top_logit)
    total_sum = jnp.sum(exponent_values, axis=1, keepdims=True)
    return (
        exponent_values / total_sum,
        SOFTMAX_TEMP * (top_logit[:, 0] + jnp.log(total_sum[:, 0])),
    )


def local(points, coarse, candidates, centroids):
    groups = lax.axis_size("grp")
    members = lax.axis_size("dev")
    tok_rows, width = points.shape
    clusters_all = candidates.shape[0]
    per_group = clusters_all // groups
    capacity = 2 * tok_rows // clusters_all
    per_member = capacity // members
    label = coarse[:, 0]
    onehot = (label[:, None] == jnp.arange(clusters_all, dtype=jnp.int32)[None, :]).astype(
        jnp.int32
    )
    ranking = jnp.sum((jnp.cumsum(onehot, axis=0) - onehot) * onehot, axis=1)
    owner = label // per_group
    local_id = label % per_group
    target = (
        (local_id * groups + owner) * members + ranking % members
    ) * per_member + ranking // members
    slot_count = per_group * groups * members * per_member
    send_rows = jnp.zeros((slot_count, width), jnp.bfloat16).at[target].set(points)
    send_live = jnp.zeros((slot_count,), jnp.int32).at[target].set(1)
    got_rows, got_live = (
        lax.all_to_all(
            send_rows.reshape(per_group, groups * members, per_member, width),
            ("grp", "dev"),
            split_axis=1,
            concat_axis=1,
            tiled=True,
        ),
        lax.all_to_all(
            send_live.reshape(per_group, groups * members, per_member),
            ("grp", "dev"),
            split_axis=1,
            concat_axis=1,
            tiled=True,
        ),
    )
    rows = got_rows.reshape(per_group, -1, width)
    live = got_live.reshape(per_group, -1).astype(jnp.float32)
    group_pool = lax.all_gather(centroids, "dev", axis=0, tiled=True)
    pool_size = group_pool.shape[0]
    squared_norms = jnp.sum(jnp.square(group_pool.astype(jnp.float32)), axis=1)
    mine = lax.axis_index("grp")
    local_lists = lax.dynamic_slice_in_dim(candidates, mine * per_group, per_group, 0)
    affinity_parts = []
    block_ids = jnp.arange(pool_size, dtype=jnp.int32) // BLK
    sums = jnp.zeros((pool_size, width), jnp.float32)
    weight_total = jnp.zeros((pool_size,), jnp.float32)
    for cluster in range(per_group):
        allowed_mask = jnp.any(block_ids[None, :] == local_lists[cluster][:, None], axis=0)
        inner_products = jnp.einsum(
            "rd,kd->rk", rows[cluster], group_pool, preferred_element_type=jnp.float32
        )
        logit_scores = jnp.where(
            allowed_mask[None, :],
            (2.0 * inner_products - squared_norms[None, :]) / SOFTMAX_TEMP,
            -jnp.inf,
        )
        probs, cluster_affinity = softmax_parts(logit_scores)
        weights = (probs * live[cluster][:, None]).astype(jnp.bfloat16)
        sums = sums + jnp.einsum(
            "rk,rd->kd", weights, rows[cluster], preferred_element_type=jnp.float32
        )
        weight_total = weight_total + jnp.sum(weights.astype(jnp.float32), axis=0)
        affinity_parts.append(cluster_affinity)
    mine_sums, mine_weights = (
        lax.psum_scatter(sums, "dev", scatter_dimension=0, tiled=True),
        lax.psum_scatter(weight_total, "dev", scatter_dimension=0, tiled=True),
    )
    updated = (mine_sums + PRIOR_WEIGHT * centroids.astype(jnp.float32)) / (
        mine_weights + PRIOR_WEIGHT
    )[:, None]
    affinity_slots = jnp.stack(affinity_parts)
    returned = lax.all_to_all(
        affinity_slots.reshape(per_group, groups * members, per_member),
        ("grp", "dev"),
        split_axis=1,
        concat_axis=1,
        tiled=True,
    )
    point_affinity = returned.reshape(-1)[target]
    return (updated, point_affinity)


def solution(mesh):
    return jax.shard_map(
        local,
        mesh=mesh,
        in_specs=(P(("grp", "dev"), None), P(("grp", "dev"), None), P(), P(("grp", "dev"), None)),
        out_specs=(P(("grp", "dev"), None), P(("grp", "dev"))),
        check_vma=False,
    )
```

profile of v0, /device:TPU:1, one launch (start us, length us, event | category | flops | bytes accessed | tf_op | source)
XLA Modules:
  0.0 183.6 jit_solution(13169817412623778063)
XLA Ops:
  7.2 0.0 copy-start
  7.2 0.0 all-gather.2.cloned.1.call-start
  7.2 0.7 all-gather.2.cloned.1.call-update
  7.9 0.7 fusion.21
  8.6 1.2 reduce-window.6
  9.8 0.2 slice_reduce_fusion.4
  10.0 0.8 fusion.20
  10.8 0.7 compare_select_fusion
  11.6 2.4 %scatter_custom_fusion.1 = s32[1024]{0:T(1024)S(1)} fusion(s32[512]{0:T(512)S(1)} %bitcast.52, s32[512]{0:T(512)S(1)} %broadcast.230, s32[]{:T(128)} %constant.83.clone.1), kind=kCustom, calls=%fused_computation.85 | custom fusion | bytes 4100 | tf_op jit(solution)/shard_map/scatter | solution.py:43
  14.0 0.2 reshape.277
  14.2 1.5 copy.18
  15.7 11.5 %all-to-all-start.1 = ((s32[4,128,2]{0,2,1:T(2,128)}), s32[4,128,2]{0,2,1:T(2,128)S(1)}, u32[]{:S(2)}, u32[]{:S(2)}) async-start(s32[4,128,2]{0,2,1:T(2,128)} %copy.18), calls=%async_computation.1 | async-start | bytes 262144 | tf_op jit(solution)/shard_map/all_to_all | solution.py:52
  27.2 3.9 %scatter_custom_fusion = bf16[1024,1024]{1,0:T(8,128)(2,1)S(1)} fusion(s32[512]{0:T(512)S(1)} %bitcast.53, bf16[512,1024]{1,0:T(8,128)(2,1)} %param.4, bf16[]{:T(256)} %constant.91.clone.1), kind=kCustom, calls=%fused_computation.33 | custom fusion | bytes 2097664 | tf_op jit(solution)/shard_map/scatter | solution.py:42
  31.1 2.3 %reshape.276 = bf16[4,128,2,1024]{3,2,1,0:T(2,128)(2,1)} reshape(bf16[1024,1024]{1,0:T(8,128)(2,1)S(1)} %scatter_custom_fusion) | data formatting | bytes 4194304 | tf_op jit(solution)/shard_map/reshape | solution.py:46
  33.4 5.3 %copy.17 = bf16[4,128,2,1024]{3,2,0,1:T(2,128)(2,1)} copy(bf16[4,128,2,1024]{3,2,1,0:T(2,128)(2,1)} %reshape.276) | data formatting | bytes 4194304 | tf_op jit(solution)/shard_map/reshape | solution.py:46
  38.7 9.8 %all-to-all-start = ((bf16[4,128,2,1024]{3,2,0,1:T(2,128)(2,1)}), bf16[4,128,2,1024]{3,2,0,1:T(2,128)(2,1)S(1)}, u32[]{:S(2)}, u32[]{:S(2)}) async-start(bf16[4,128,2,1024]{3,2,0,1:T(2,128)(2,1)} %copy.17), calls=%async_computation | async-start | bytes 4194304 | tf_op jit(solution)/shard_map/all_to_all | solution.py:45
  48.5 0.0 reduce-scatter.2.cloned.1.call-start
  48.5 0.1 constant_dynamic-slice_fusion
  48.6 0.2 slice_reduce_fusion.5
  48.8 0.1 compare_reduce_fusion
  49.0 1.0 slice_reduce_fusion
  50.1 0.1 mul.153
  50.2 0.1 mul.149
  50.3 0.1 mul.145
  50.5 0.1 mul.141
  50.6 31.0 %all-to-all-done = bf16[4,128,2,1024]{3,2,0,1:T(2,128)(2,1)S(1)} async-done(((bf16[4,128,2,1024]{3,2,0,1:T(2,128)(2,1)}), bf16[4,128,2,1024]{3,2,0,1:T(2,128)(2,1)S(1)}, u32[]{:S(2)}, u32[]{:S(2)}) %all-to-all-start) | async-done | bytes 2097184 | tf_op jit(solution)/shard_map/all_to_all | solution.py:45
  81.6 2.9 %fusion.30 = (bf16[1,128,2,1024]{3,2,0,1:T(2,128)(2,1)}, bf16[1,128,2,1024]{3,2,0,1:T(2,128)(2,1)}, bf16[1,128,2,1024]{3,2,0,1:T(2,128)(2,1)S(1)}, bf16[1,128,2,1024]{3,2,0,1:T(2,128)(2,1)S(1)}) fusion(bf16[4,128,2,1024]{3,2,0,1:T(2,128)(2,1)S(1)} %all-to-all-done), kind=kLoop, calls=%fused_computation.93 | loop fusion | bytes 4194304 | tf_op jit(solution)/shard_map/slice | solution.py:74
  84.5 1.2 squeeze.20
  85.7 1.2 squeeze.19
  87.0 0.2 squeeze.18
  87.2 0.2 squeeze.8
  87.4 0.0 all-gather.2.cloned.1.call-done
  87.4 2.2 %multiply_reduce_fusion = f32[1024]{0:T(1024)S(1)} fusion(bf16[1024,1024]{1,0:T(8,128)(2,1)} %all-gather.2.cloned.1.call-done), kind=kLoop, calls=%fused_computation.4 | loop fusion | flops 3144704 | bytes 2101248 | tf_op jit(solution)/shard_map/reduce_sum | solution.py:64
  89.7 0.9 fusion.31
  90.6 0.3 fusion.16
  90.9 0.9 fusion.34
  91.8 0.3 fusion.17
  92.2 0.6 convert_reduce_fusion
  92.8 0.7 fusion.37
  93.6 0.9 fusion.32
  94.5 0.3 fusion.14
  94.8 0.9 fusion.33
  95.8 0.3 fusion.15
  96.1 0.6 convert_reduce_fusion.2
  96.7 0.7 fusion.36
  97.5 0.7 fusion.35
  98.2 2.7 %add_add_fusion = f32[1024,1024]{1,0:T(8,128)} fusion(f32[1024,1024]{1,0:T(8,128)S(1)} %fusion.37, f32[1024,1024]{1,0:T(8,128)S(1)} %fusion.35, f32[1024,1024]{1,0:T(8,128)S(1)} %fusion.36, bf16[256,1024]{1,0:T(8,128)(2,1)S(1)} %get-tuple-element.21, bf16[256,1024]{1,0:T(8,128)(2,1)S(1)} %squeeze.20), kind=kOutput, calls=%fused_computation.3 | convolution fusion | flops 540016640 | bytes 17825792 | tf_op jit(solution)/shard_map/rk,rd->kd/dot_general | solution.py:83
  101.0 0.0 reduce-scatter.2.cloned.1.call-update
  101.0 0.6 copy-done.3
  101.6 0.6 dynamic-slice
  102.9 0.1 mul.157
  103.0 0.0 copy-start.2
  103.1 0.1 mul.159
  103.2 0.1 mul.163
  103.4 0.1 mul.161
  103.5 1.5 copy.19
  105.1 5.3 %all-to-all-start.2 = ((f32[4,128,2]{0,2,1:T(2,128)}), f32[4,128,2]{0,2,1:T(2,128)S(1)}, u32[]{:S(2)}, u32[]{:S(2)}) async-start(f32[4,128,2]{0,2,1:T(2,128)} %copy.19), calls=%async_computation.3 | async-start | bytes 262144 | tf_op jit(solution)/shard_map/all_to_all | solution.py:96
  110.4 34.3 %all-reduce = f32[1024]{0:T(1024)S(1)} all-reduce(f32[1024]{0:T(1024)S(1)} %add_add_fusion.1), channel_id=3, replica_groups=mesh['grp'=8,'dev'=16] {'dev'}, use_global_device_ids=true, to_apply=%region_23.24.clone | all-reduce | flops 1024 | bytes 8192
  144.7 0.1 dynamic-slice_add_fusion
  144.8 1.0 copy.20
  145.8 0.2 reshape.278
  146.0 3.4 %gather_fusion = f32[512]{0:T(512)} fusion(f32[1024]{0:T(1024)S(1)} %reshape.278, s32[1024]{0:T(1024)S(1)} %pad_clamp_fusion), kind=kCustom, calls=%fused_computation | custom fusion | bytes 6144 | tf_op jit(solution)/shard_map/gather | solution.py:103
  149.4 25.6 %reduce-scatter.2.cloned.1.call-done = f32[64,1024]{1,0:T(8,128)} async-done(((f32[1024,1024]{1,0:T(8,128)}), f32[64,1024]{1,0:T(8,128)}) %reduce-scatter.2.cloned.1.call-update) | async-done | bytes 262160 | tf_op jit(solution)/shard_map/reduce_scatter | solution.py:89
  175.0 1.7 add_divide_fusion
  (19 shorter events, 0.2 us)
Async XLA Ops:
  7.2 41.3 %copy-start = (s32[32,4]{0,1:T(4,128)S(1)}, s32[32,4]{0,1:T(4,128)}, u32[]{:S(2)}) copy-start(s32[32,4]{0,1:T(4,128)} %param.6) | copy-start | bytes 1540
  7.2 80.2 %all-gather.2.cloned.1.call-start = ((), (), s32[]{:S(2)}) async-start(), calls=%async_computation.4 | async-start | bytes 2228224 | tf_op jit(solution)/shard_map/all_gather | solution.py:62
  15.7 23.0 %all-to-all-start.1 = ((s32[4,128,2]{0,2,1:T(2,128)}), s32[4,128,2]{0,2,1:T(2,128)S(1)}, u32[]{:S(2)}, u32[]{:S(2)}) async-start(s32[4,128,2]{0,2,1:T(2,128)} %copy.18), calls=%async_computation.1 | async-start | bytes 262144 | tf_op jit(solution)/shard_map/all_to_all | solution.py:52
  38.7 42.9 %all-to-all-start = ((bf16[4,128,2,1024]{3,2,0,1:T(2,128)(2,1)}), bf16[4,128,2,1024]{3,2,0,1:T(2,128)(2,1)S(1)}, u32[]{:S(2)}, u32[]{:S(2)}) async-start(bf16[4,128,2,1024]{3,2,0,1:T(2,128)(2,1)} %copy.17), calls=%async_computation | async-start | bytes 4194304 | tf_op jit(solution)/shard_map/all_to_all | solution.py:45
  48.5 126.6 %reduce-scatter.2.cloned.1.call-start = ((), (), s32[]{:S(2)}) async-start(), calls=%async_computation.5 | async-start | bytes 4456448 | tf_op jit(solution)/shard_map/reduce_scatter | solution.py:89
  87.4 2.2 %copy-start.1 = (bf16[1024,1024]{1,0:T(8,128)(2,1)S(1)}, bf16[1024,1024]{1,0:T(8,128)(2,1)}, u32[]{:S(2)}) copy-start(bf16[1024,1024]{1,0:T(8,128)(2,1)} %all-gather.2.cloned.1.call-done) | copy-start | bytes 6291460
  101.0 0.7 copy-start.3
  103.0 72.0 %copy-start.2 = (bf16[64,1024]{1,0:T(8,128)(2,1)S(1)}, bf16[64,1024]{1,0:T(8,128)(2,1)}, u32[]{:S(2)}) copy-start(bf16[64,1024]{1,0:T(8,128)(2,1)} %param.7) | copy-start | bytes 393220
  105.1 39.8 %all-to-all-start.2 = ((f32[4,128,2]{0,2,1:T(2,128)}), f32[4,128,2]{0,2,1:T(2,128)S(1)}, u32[]{:S(2)}, u32[]{:S(2)}) async-start(f32[4,128,2]{0,2,1:T(2,128)} %copy.19), calls=%async_computation.3 | async-start | bytes 262144 | tf_op jit(solution)/shard_map/all_to_all | solution.py:96
Sparse Core Ops, SparseCore 0:
  10.2 69.8 all-gather.1
  101.1 73.8 reduce-scatter.1
where the time goes:
time: 185 us; the launch traced here: 184 us
  waiting for transfers between devices  57.3 us (31%)
  blocking collectives  34.3 us (19%)
  local copies, waits for them, and re-layouts  31.4 us (17%)
  starting transfers between devices  26.7 us (14%)
  between operations  15 us (8%)
  other arithmetic  10.2 us (6%)
  matrix products  8.76 us (5%)
    unnamed x1, blocking collectives  34.3 us
    all_to_all x1, waiting for transfers between devices, local(): lax.all_to_all(send_rows.reshape(per_group, groups * members, per_member,...  31 us
    reduce_scatter x1, waiting for transfers between devices, local(): lax.psum_scatter(sums, 'dev', scatter_dimension=0, tiled=True)  25.6 us
    all_to_all x1, starting transfers between devices, local(): lax.all_to_all(send_live.reshape(per_group, groups * members, per_member)...  11.5 us
    all_to_all x1, starting transfers between devices, local(): lax.all_to_all(send_rows.reshape(per_group, groups * members, per_member,...  9.75 us
    reshape x2, local copies, waits for them, and re-layouts, local(): send_rows.reshape(per_group, groups * members, per_member, width)  7.55 us
    all_to_all x1, starting transfers between devices, local(): lax.all_to_all(affinity_slots.reshape(per_group, groups * members, per_me...  5.35 us
    dot_general x4, matrix products, local(): jnp.einsum('rk,rd->kd', weights, rows[cluster], preferred_element_type=jn...  4.99 us
  transfers between devices with their start and end apart: 5, of which 2 were waited for; matrix products, arithmetic and copies ran while one was open for 19% of the time, Pallas kernels for 0%

commit v1 on v0

v1 whole, which is shorter than its diff:
```python
import functools

import jax
import jax.numpy as jnp
from jax import lax
from jax.experimental import pallas as pl
from jax.experimental.pallas import tpu as pltpu
from jax.sharding import PartitionSpec as P

MESH = pl.DeviceIdType.MESH
F32 = jnp.float32
BF16 = jnp.bfloat16

SOFTMAX_TEMP = 0.4
PRIOR_WEIGHT = 1.0
FAR = 1e30

GROUPS = 8
MEMBERS = 16
ROWS = 512
WIDTH = 1024
SHARD = 64
POOL = MEMBERS * SHARD
PER_GROUP = 4
CLUSTERS = 32
CAP = 32
LISTED = 4
BLK = 128
SLOTS = PER_GROUP * CAP
HALF = WIDTH // 2
QUARTER = WIDTH // 4


def iota(shape, axis):
    return lax.broadcasted_iota(jnp.int32, shape, axis)


def kernel(
    cand,
    points,
    coarse,
    cent,
    new_ref,
    aff_ref,
    tx,
    rx,
    txf,
    rxf,
    pool,
    norms,
    logits,
    weights,
    afftx,
    affrx,
    tottx,
    totrx,
    part_a,
    part_b,
    own_a,
    own_b,
    far1_a,
    near1_a,
    far1_b,
    near1_b,
    send2_a,
    send2_b,
    far2_a,
    near2_a,
    far2_b,
    near2_b,
    local_sem,
    row_send,
    row_recv,
    flag_send,
    flag_recv,
    aff_send,
    aff_recv,
    tot_send,
    tot_recv,
    ag1_send,
    ag1_recv,
    ag2_send,
    ag2_recv,
    far_send,
    far_recv,
    near_send,
    near_recv,
):
    g = lax.axis_index("grp")
    d = lax.axis_index("dev")
    x, c = lax.div(g, 2), lax.rem(g, 2)
    z, y = lax.div(d, 4), lax.rem(d, 4)

    def group_at(k):
        return lax.rem(x + k // 2, 4) * 2 + lax.rem(c + k % 2, 2)

    def group_from(k):
        return lax.rem(x + 4 - k // 2, 4) * 2 + lax.rem(c + k % 2, 2)

    def turn(value, by):
        return lax.rem(value + by + 4, 4)

    def member(first, second, axis):
        return first * 4 + second if axis == 0 else second * 4 + first

    place = ((z, y), (y, z))

    barrier = pltpu.get_barrier_semaphore()
    for k in range(1, GROUPS):
        pl.semaphore_signal(barrier, inc=1, device_id=(group_at(k), d), device_id_type=MESH)
    for k in range(1, MEMBERS):
        pl.semaphore_signal(
            barrier, inc=1, device_id=(g, lax.rem(d + k, MEMBERS)), device_id_type=MESH
        )

    own_copy = pltpu.make_async_copy(cent, pool.at[d], local_sem)
    own_copy.start()
    cluster_ids = iota((CLUSTERS, ROWS), 0)
    named = (coarse[...] == cluster_ids).astype(F32)
    before = (iota((ROWS, ROWS), 0) < iota((ROWS, ROWS), 1)).astype(F32).astype(BF16)
    rank = jnp.dot(named.astype(BF16), before, preferred_element_type=F32)
    slot = jnp.sum(named * (rank + (cluster_ids * CAP).astype(F32)), axis=0, keepdims=True)
    count = jnp.sum(named, axis=1, keepdims=True)
    slot_ids = iota((SLOTS, ROWS), 0)
    lane = iota((CLUSTERS, SLOTS), 1)
    lane_cluster, lane_rank = lax.div(lane, CAP), lax.rem(lane, CAP)

    def pack(k, owner, rows_ref, flag_ref):
        here = slot == (slot_ids + owner * SLOTS).astype(F32)
        rows_ref[k] = jnp.dot(
            here.astype(F32).astype(BF16), points[...], preferred_element_type=F32
        ).astype(BF16)
        mine = iota((CLUSTERS, SLOTS), 0) == lane_cluster + owner * PER_GROUP
        held = jnp.sum(jnp.where(mine, count, 0.0), axis=0, keepdims=True)
        live = (lane_rank[0:1].astype(F32) < held).astype(F32)
        flag_ref[k] = jnp.broadcast_to(live, (8, SLOTS))

    def row_copy(k):
        return pltpu.make_async_remote_copy(
            src_ref=tx.at[k],
            dst_ref=rx.at[k],
            send_sem=row_send.at[k],
            recv_sem=row_recv.at[k],
            device_id=(group_at(k), d),
            device_id_type=MESH,
        )

    def flag_copy(k):
        return pltpu.make_async_remote_copy(
            src_ref=txf.at[k],
            dst_ref=rxf.at[k],
            send_sem=flag_send.at[k],
            recv_sem=flag_recv.at[k],
            device_id=(group_at(k), d),
            device_id_type=MESH,
        )

    def columns(axis):
        return pl.ds(axis * HALF, HALF)

    def gather1(axis, k):
        first, second = place[axis]
        piece = pool.at[d, :, columns(axis)]
        return pltpu.make_async_remote_copy(
            src_ref=piece,
            dst_ref=piece,
            send_sem=ag1_send.at[axis, k],
            recv_sem=ag1_recv.at[axis, k],
            device_id=(g, member(turn(first, k), second, axis)),
            device_id_type=MESH,
        )

    def gather2(axis, k1, k2):
        first, second = place[axis]
        piece = pool.at[member(turn(first, -k1), second, axis), :, columns(axis)]
        return pltpu.make_async_remote_copy(
            src_ref=piece,
            dst_ref=piece,
            send_sem=ag2_send.at[axis, k1, k2],
            recv_sem=ag2_recv.at[axis, k1, k2],
            device_id=(g, member(first, turn(second, k2), axis)),
            device_id_type=MESH,
        )

    own_copy.wait()
    pl.semaphore_wait(barrier, GROUPS - 1 + MEMBERS - 1)
    for axis in (0, 1):
        for k in (2, 1, 3):
            gather1(axis, k).start()
    for k in (4, 5, 2, 6, 3, 7, 1):
        pack(k, group_at(k), tx, txf)
        flag_copy(k).start()
        row_copy(k).start()
        if k == 2:
            for axis in (0, 1):
                for k2 in (2, 1, 3):
                    gather2(axis, 0, k2).start()
    pack(0, g, rx, rxf)

    for k1 in (1, 3, 2):
        for axis in (0, 1):
            gather1(axis, k1).wait_recv()
            for k2 in (2, 1, 3):
                gather2(axis, k1, k2).start()

    block = iota((8, SLOTS), 0)
    allowed = jnp.zeros((8, SLOTS), jnp.bool_)
    wide_cluster = lax.div(iota((8, SLOTS), 1), CAP)
    for cluster in range(PER_GROUP):
        for j in range(LISTED):
            listed = cand[j, g * PER_GROUP + cluster]
            allowed = allowed | ((block == listed) & (wide_cluster == cluster))
    penalty = jnp.where(allowed, 0.0, FAR)

    for axis in (0, 1):
        for k1 in range(4):
            for k2 in range(1, 4):
                gather2(axis, k1, k2).wait_recv()

    for b in range(8):
        rows = pool[2 * b : 2 * b + 2].reshape(BLK, WIDTH).astype(F32)
        square = jnp.sum(rows * rows, axis=1, keepdims=True)
        norms[b] = square + penalty[b : b + 1]

    def aff_copy(k):
        return pltpu.make_async_remote_copy(
            src_ref=afftx.at[k],
            dst_ref=affrx.at[k],
            send_sem=aff_send.at[k],
            recv_sem=aff_recv.at[k],
            device_id=(group_from(k), d),
            device_id_type=MESH,
        )

    def score(pair):
        for k in (2 * pair, 2 * pair + 1):
            if k:
                flag_copy(k).wait_recv()
                row_copy(k).wait_recv()
        rows = rx[2 * pair : 2 * pair + 2].reshape(2 * SLOTS, WIDTH)
        live = jnp.concatenate([rxf[2 * pair, 0:1], rxf[2 * pair + 1, 0:1]], axis=1)

        def first(t, top):
            tile = pool[pl.ds(4 * t, 4)].reshape(4 * SHARD, WIDTH)
            inner = lax.dot_general(
                tile, rows, (((1,), (1,)), ((), ())), preferred_element_type=F32
            )
            square = norms[pl.ds(2 * t, 2)].reshape(4 * SHARD, SLOTS)
            value = (2.0 * inner - jnp.concatenate([square, square], axis=1)) * (
                1.0 / SOFTMAX_TEMP
            )
            logits[t] = value
            return jnp.maximum(top, jnp.max(value, axis=0, keepdims=True))

        top = lax.fori_loop(0, 4, first, jnp.full((1, 2 * SLOTS), -jnp.inf, F32))

        def second(t, total):
            value = jnp.exp(logits[t] - top)
            logits[t] = value
            return total + jnp.sum(value, axis=0, keepdims=True)

        total = lax.fori_loop(0, 4, second, jnp.zeros((1, 2 * SLOTS), F32))
        scale = live / total

        def third(t, carry):
            weights[pl.ds(4 * t, 4), :, pl.ds(2 * pair * SLOTS, 2 * SLOTS)] = (
                (logits[t] * scale).astype(BF16).reshape(4, SHARD, 2 * SLOTS)
            )
            return carry

        lax.fori_loop(0, 4, third, 0)
        affinity = SOFTMAX_TEMP * (top + jnp.log(total))
        for i, k in enumerate((2 * pair, 2 * pair + 1)):
            mine = jnp.broadcast_to(affinity[:, i * SLOTS : (i + 1) * SLOTS], (8, SLOTS))
            if k:
                afftx[k] = mine
                aff_copy(k).start()
            else:
                affrx[0] = mine

    for pair in (0, 1, 3, 2):
        score(pair)

    part = (part_a, part_b)
    own = (own_a, own_b)
    far1, near1 = (far1_a, far1_b), (near1_a, near1_b)
    send2 = (send2_a, send2_b)
    far2, near2 = (far2_a, far2_b), (near2_a, near2_b)

    def product(axis, index):
        if axis == 0:
            lhs = weights[pl.ds(4 * index, 4)].reshape(4 * SHARD, POOL)
        else:
            lhs = jnp.concatenate([weights[4 * i + index] for i in range(4)], axis=0)
        rhs = rx[:, :, axis * HALF : (axis + 1) * HALF].reshape(GROUPS * SLOTS, HALF)
        return jnp.dot(lhs, rhs, preferred_element_type=F32)

    def hop(phase, axis, side, near, part_index):
        first, second = place[axis]
        step = 1 - 2 * side
        if phase == 0:
            target = member(turn(first, step), second, axis)
            source = part[axis].at[turn(first, step if near else 2)]
        else:
            target = member(first, turn(second, step), axis)
            source = send2[axis].at[turn(second, step if near else 2)]
        piece = pl.ds(part_index * QUARTER, QUARTER)
        if near:
            landing = (near1, near2)[phase][axis].at[side, :, piece]
            semaphores = near_send.at[phase, axis, side, part_index], near_recv.at[
                phase, axis, side, part_index
            ]
        else:
            landing = (far1, far2)[phase][axis].at[side]
            semaphores = far_send.at[phase, axis, side], far_recv.at[phase, axis, side]
        return pltpu.make_async_remote_copy(
            src_ref=source.at[:, piece],
            dst_ref=landing,
            send_sem=semaphores[0],
            recv_sem=semaphores[1],
            device_id=(g, target),
            device_id_type=MESH,
        )

    def add_far(phase, axis, side):
        first, second = place[axis]
        buffer = (part, send2)[phase][axis]
        landing = (far1, far2)[phase][axis]
        index = turn((first, second)[phase], 1 - 2 * side)
        hop(phase, axis, side, False, side).wait_recv()
        piece = slice(side * QUARTER, (side + 1) * QUARTER)
        buffer[index, :, piece] = (
            buffer[index, :, piece].astype(F32) + landing[side].astype(F32)
        ).astype(BF16)
        hop(phase, axis, side, True, side).start()

    for axis in (0, 1):
        index = turn(place[axis][0], 2)
        part[axis][index] = product(axis, index).astype(BF16)
        for side in (0, 1):
            hop(0, axis, side, False, side).start()
    for axis in (0, 1):
        for side in (0, 1):
            index = turn(place[axis][0], 1 - 2 * side)
            part[axis][index] = product(axis, index).astype(BF16)
            hop(0, axis, side, True, 1 - side).start()

    lanes = iota((SHARD, BLK), 1)
    diagonal = lanes == iota((SHARD, BLK), 0)

    def total_copy(k):
        return pltpu.make_async_remote_copy(
            src_ref=tottx.at[lax.rem(d + k, MEMBERS)],
            dst_ref=totrx.at[k],
            send_sem=tot_send.at[k],
            recv_sem=tot_recv.at[k],
            device_id=(g, lax.rem(d + k, MEMBERS)),
            device_id_type=MESH,
        )

    def total_of(i, carry):
        column = jnp.sum(weights[i].astype(F32), axis=1, keepdims=True)
        row = jnp.sum(jnp.where(diagonal, column, 0.0), axis=0, keepdims=True)
        tottx[i] = jnp.broadcast_to(row, (8, BLK))
        return carry

    lax.fori_loop(0, MEMBERS, total_of, 0)
    for k in range(1, MEMBERS):
        total_copy(k).start()

    for axis in (0, 1):
        for side in (0, 1):
            add_far(0, axis, side)
    for axis in (0, 1):
        own[axis][...] = product(axis, place[axis][0])

    affinity = jnp.zeros((1, ROWS), F32)
    square_eye = iota((SLOTS, SLOTS), 0) == iota((SLOTS, SLOTS), 1)
    for k in range(GROUPS):
        if k:
            aff_copy(k).wait_recv()
        column = jnp.sum(jnp.where(square_eye, affrx[k, 0:1], 0.0), axis=1, keepdims=True)
        here = slot == (slot_ids + group_at(k) * SLOTS).astype(F32)
        affinity = affinity + jnp.sum(jnp.where(here, column, 0.0), axis=0, keepdims=True)
    aff_ref[...] = affinity

    for axis in (0, 1):
        total = own[axis][...]
        for side in (0, 1):
            for piece in (0, 1):
                hop(0, axis, side, True, piece).wait_recv()
            total = total + near1[axis][side].astype(F32)
        own[axis][...] = total
        send2[axis][...] = total.astype(BF16).reshape(4, SHARD, HALF)
        for side in (0, 1):
            hop(1, axis, side, False, side).start()
        for side in (0, 1):
            hop(1, axis, side, True, 1 - side).start()
    for axis in (0, 1):
        for side in (0, 1):
            add_far(1, axis, side)

    totals = tottx[d]
    for k in range(1, MEMBERS):
        total_copy(k).wait_recv()
        totals = totals + totrx[k]
    column = jnp.sum(jnp.where(diagonal, totals[0:1], 0.0), axis=1, keepdims=True)

    for axis in (0, 1):
        mine = own[axis][pl.ds(place[axis][1] * SHARD, SHARD)]
        for side in (0, 1):
            for piece in (0, 1):
                hop(1, axis, side, True, piece).wait_recv()
            mine = mine + near2[axis][side].astype(F32)
        span = slice(axis * HALF, (axis + 1) * HALF)
        new_ref[:, span] = (mine + PRIOR_WEIGHT * cent[:, span].astype(F32)) / (
            column + PRIOR_WEIGHT
        )

    for k in range(1, GROUPS):
        flag_copy(k).wait_send()
        row_copy(k).wait_send()
        aff_copy(k).wait_send()
    for k in range(1, MEMBERS):
        total_copy(k).wait_send()
    for axis in (0, 1):
        for k in range(1, 4):
            gather1(axis, k).wait_send()
            for k1 in range(4):
                gather2(axis, k1, k).wait_send()
        for phase in (0, 1):
            for side in (0, 1):
                hop(phase, axis, side, False, side).wait_send()
                for piece in (0, 1):
                    hop(phase, axis, side, True, piece).wait_send()


def local(points, coarse, candidates, centroids):
    vmem = pl.BlockSpec(memory_space=pltpu.VMEM)
    dma = pltpu.SemaphoreType.DMA
    updated, affinity = pl.pallas_call(
        kernel,
        out_shape=(
            jax.ShapeDtypeStruct((SHARD, WIDTH), F32),
            jax.ShapeDtypeStruct((1, ROWS), F32),
        ),
        in_specs=[pl.BlockSpec(memory_space=pltpu.SMEM), vmem, vmem, vmem],
        out_specs=(vmem, vmem),
        scratch_shapes=[
            pltpu.VMEM((GROUPS, SLOTS, WIDTH), BF16),
            pltpu.VMEM((GROUPS, SLOTS, WIDTH), BF16),
            pltpu.VMEM((GROUPS, 8, SLOTS), F32),
            pltpu.VMEM((GROUPS, 8, SLOTS), F32),
            pltpu.VMEM((MEMBERS, SHARD, WIDTH), BF16),
            pltpu.VMEM((8, BLK, SLOTS), F32),
            pltpu.VMEM((4, 4 * SHARD, 2 * SLOTS), F32),
            pltpu.VMEM((MEMBERS, SHARD, GROUPS * SLOTS), BF16),
            pltpu.VMEM((GROUPS, 8, SLOTS), F32),
            pltpu.VMEM((GROUPS, 8, SLOTS), F32),
            pltpu.VMEM((MEMBERS, 8, BLK), F32),
            pltpu.VMEM((MEMBERS, 8, BLK), F32),
            pltpu.VMEM((4, 4 * SHARD, HALF), BF16),
            pltpu.VMEM((4, 4 * SHARD, HALF), BF16),
            pltpu.VMEM((4 * SHARD, HALF), F32),
            pltpu.VMEM((4 * SHARD, HALF), F32),
            pltpu.VMEM((2, 4 * SHARD, QUARTER), BF16),
            pltpu.VMEM((2, 4 * SHARD, HALF), BF16),
            pltpu.VMEM((2, 4 * SHARD, QUARTER), BF16),
            pltpu.VMEM((2, 4 * SHARD, HALF), BF16),
            pltpu.VMEM((4, SHARD, HALF), BF16),
            pltpu.VMEM((4, SHARD, HALF), BF16),
            pltpu.VMEM((2, SHARD, QUARTER), BF16),
            pltpu.VMEM((2, SHARD, HALF), BF16),
            pltpu.VMEM((2, SHARD, QUARTER), BF16),
            pltpu.VMEM((2, SHARD, HALF), BF16),
            dma,
            dma((GROUPS,)),
            dma((GROUPS,)),
            dma((GROUPS,)),
            dma((GROUPS,)),
            dma((GROUPS,)),
            dma((GROUPS,)),
            dma((MEMBERS,)),
            dma((MEMBERS,)),
            dma((2, 4)),
            dma((2, 4)),
            dma((2, 4, 4)),
            dma((2, 4, 4)),
            dma((2, 2, 2)),
            dma((2, 2, 2)),
            dma((2, 2, 2, 2)),
            dma((2, 2, 2, 2)),
        ],
        compiler_params=pltpu.CompilerParams(
            collective_id=0, has_side_effects=True, vmem_limit_bytes=40 << 20
        ),
    )(candidates.T, points, coarse.reshape(1, ROWS), centroids)
    return updated, affinity.reshape(ROWS)


def solution(mesh):
    return jax.shard_map(
        local,
        mesh=mesh,
        in_specs=(P(("grp", "dev"), None), P(("grp", "dev"), None), P(), P(("grp", "dev"), None)),
        out_specs=(P(("grp", "dev"), None), P(("grp", "dev"))),
        check_vma=False,
    )
```

time: 185 us -> 65.5 us (0.35)
  the two profiles are of different devices: /device:TPU:1 before, /device:TPU:0 now
where the time goes in v1:
time: 65.5 us; the launch traced here: 65.3 us
  Pallas kernels  59.8 us (91%)
  local copies, waits for them, and re-layouts  4.77 us (7%)
    pallas_call x1, Pallas kernels, local(): pl.pallas_call(kernel, out_shape=(jax.ShapeDtypeStruct((SHARD, WIDTH), F3...  59.8 us
    unnamed x10, local copies, waits for them, and re-layouts  4.77 us

profile of v1, /device:TPU:0, one launch (start us, length us, event | category | flops | bytes accessed | tf_op | source)
XLA Modules:
  0.0 65.3 jit_solution(10604587302460661073)
XLA Ops:
  0.6 0.0 copy-start.2
  0.6 0.7 %copy-done.2 = s32[32,4]{0,1:T(4,128)S(1)} copy-done((s32[32,4]{0,1:T(4,128)S(1)}, s32[32,4]{0,1:T(4,128)}, u32[]{:S(2)}) %copy-start.2) | copy-done | bytes 536
  1.3 0.0 copy-start
  1.3 1.2 %copy-done = bf16[512,1024]{1,0:T(8,128)(2,1)S(1)} copy-done((bf16[512,1024]{1,0:T(8,128)(2,1)S(1)}, bf16[512,1024]{1,0:T(8,128)(2,1)}, u32[]{:S(2)}) %copy-start) | copy-done | bytes 1048600
  2.5 0.0 copy-start.1
  2.5 0.9 %copy-done.1 = bf16[64,1024]{1,0:T(8,128)(2,1)S(1)} copy-done((bf16[64,1024]{1,0:T(8,128)(2,1)S(1)}, bf16[64,1024]{1,0:T(8,128)(2,1)}, u32[]{:S(2)}) %copy-start.1) | copy-done | bytes 131096
  3.4 0.0 copy-start.3
  3.4 0.7 %copy-done.3 = s32[512,1]{0,1:T(1,128)S(1)} copy-done((s32[512,1]{0,1:T(1,128)S(1)}, s32[512,1]{0,1:T(1,128)}, u32[]{:S(2)}) %copy-start.3) | copy-done | bytes 2072
  4.1 59.8 %shard_map.59 = (f32[64,1024]{1,0:T(8,128)S(1)}, f32[1,512]{1,0:T(1,128)S(1)}) custom-call(s32[4,32]{1,0:T(4,128)S(1)} %bitcast.3, bf16[512,1024]{1,0:T(8,128)(2,1)S(1)} %copy-done, s32[1,512]{1,0:T(1,128)S(1)} %bitcast.4, bf16[64,1024]{1,0:T(8,128)(2,1)S(1)} %copy-done.1), custom_call_target="tpu_custom_call" | custom-call | tf_op jit(solution)/shard_map/pallas_call | solution.py:441
  64.0 0.7 %copy.8 = f32[64,1024]{1,0:T(8,128)} copy(f32[64,1024]{1,0:T(8,128)S(1)} %get-tuple-element.8) | data formatting | bytes 524288
  64.7 0.6 copy.9
Async XLA Ops:
  0.6 0.7 %copy-start.2 = (s32[32,4]{0,1:T(4,128)S(1)}, s32[32,4]{0,1:T(4,128)}, u32[]{:S(2)}) copy-start(s32[32,4]{0,1:T(4,128)} %param.6) | copy-start | bytes 1540
  1.3 1.2 %copy-start = (bf16[512,1024]{1,0:T(8,128)(2,1)S(1)}, bf16[512,1024]{1,0:T(8,128)(2,1)}, u32[]{:S(2)}) copy-start(bf16[512,1024]{1,0:T(8,128)(2,1)} %points.1) | copy-start | bytes 3145732
  2.5 0.9 %copy-start.1 = (bf16[64,1024]{1,0:T(8,128)(2,1)S(1)}, bf16[64,1024]{1,0:T(8,128)(2,1)}, u32[]{:S(2)}) copy-start(bf16[64,1024]{1,0:T(8,128)(2,1)} %cent.1) | copy-start | bytes 393220
  3.4 0.7 %copy-start.3 = (s32[512,1]{0,1:T(1,128)S(1)}, s32[512,1]{0,1:T(1,128)}, u32[]{:S(2)}) copy-start(s32[512,1]{0,1:T(1,128)} %param.5) | copy-start | bytes 6148

commit v2 on v1

v2 whole, which is shorter than its diff:
```python
import jax
import jax.numpy as jnp
from jax import lax
from jax.experimental import pallas as pl
from jax.experimental.pallas import tpu as pltpu
from jax.sharding import PartitionSpec as P

MESH = pl.DeviceIdType.MESH
F32 = jnp.float32
BF16 = jnp.bfloat16

SOFTMAX_TEMP = 0.4
PRIOR_WEIGHT = 1.0
FAR = 1e30

GROUPS = 8
MEMBERS = 16
ROWS = 512
WIDTH = 1024
SHARD = 64
POOL = MEMBERS * SHARD
PER_GROUP = 4
CLUSTERS = 32
CAP = 32
LISTED = 4
BLK = 128
SLOTS = PER_GROUP * CAP
HALF = WIDTH // 2
QUARTER = WIDTH // 4
SUBS = 2
SUB = SHARD // SUBS
ORDER = (4, 5, 2, 6, 3, 7, 1)
PAIRS = ((0, 1), (4, 5), (2, 6), (3, 7))


def iota(shape, axis):
    return lax.broadcasted_iota(jnp.int32, shape, axis)


def kernel(
    cand_hbm,
    points_hbm,
    coarse_hbm,
    cent_hbm,
    new_ref,
    aff_ref,
    cand,
    points,
    coarse,
    tx,
    rx,
    txf,
    rxf,
    pool,
    norms,
    logits,
    weights,
    afftx,
    affrx,
    tot1,
    tot1rx,
    tot2,
    tot2rx,
    part_a,
    part_b,
    own_a,
    own_b,
    far_a,
    far_b,
    near_a,
    near_b,
    send_a,
    send_b,
    last_a,
    last_b,
    in_sem,
    row_send,
    row_recv,
    flag_send,
    flag_recv,
    aff_send,
    aff_recv,
    tot_send,
    tot_recv,
    ag1_send,
    ag1_recv,
    ag2_send,
    ag2_recv,
    far_send,
    far_recv,
    near_send,
    near_recv,
    last_send,
    last_recv,
):
    g = lax.axis_index("grp")
    d = lax.axis_index("dev")
    x, c = lax.div(g, 2), lax.rem(g, 2)
    z, y = lax.div(d, 4), lax.rem(d, 4)

    def group_at(k):
        return lax.rem(x + k // 2, 4) * 2 + lax.rem(c + k % 2, 2)

    def group_from(k):
        return lax.rem(x + 4 - k // 2, 4) * 2 + lax.rem(c + k % 2, 2)

    def turn(value, by):
        return lax.rem(value + by + 4, 4)

    def member(first, second, axis):
        return first * 4 + second if axis == 0 else second * 4 + first

    place = ((z, y), (y, z))

    def remote(src, dst, send_sem, recv_sem, device):
        return pltpu.make_async_remote_copy(
            src_ref=src,
            dst_ref=dst,
            send_sem=send_sem,
            recv_sem=recv_sem,
            device_id=device,
            device_id_type=MESH,
        )

    barrier = pltpu.get_barrier_semaphore()
    for k in range(1, GROUPS):
        pl.semaphore_signal(barrier, inc=1, device_id=(group_at(k), d), device_id_type=MESH)
    for axis in (0, 1):
        first, second = place[axis]
        for k in range(1, 4):
            pl.semaphore_signal(
                barrier,
                inc=1,
                device_id=(g, member(turn(first, k), second, axis)),
                device_id_type=MESH,
            )

    coarse_in = pltpu.make_async_copy(coarse_hbm, coarse, in_sem.at[0])
    points_in = pltpu.make_async_copy(points_hbm, points, in_sem.at[1])
    cent_in = pltpu.make_async_copy(cent_hbm, pool.at[d], in_sem.at[2])
    cand_in = pltpu.make_async_copy(cand_hbm, cand, in_sem.at[3])
    coarse_in.start()
    points_in.start()
    cent_in.start()
    cand_in.start()

    cluster_ids = iota((CLUSTERS, ROWS), 0)
    before = (iota((ROWS, ROWS), 0) < iota((ROWS, ROWS), 1)).astype(F32).astype(BF16)
    coarse_in.wait()
    named = (coarse[...] == cluster_ids).astype(F32)
    rank = jnp.dot(named.astype(BF16), before, preferred_element_type=F32)
    slot = jnp.sum(named * (rank + (cluster_ids * CAP).astype(F32)), axis=0, keepdims=True)
    count = jnp.sum(named, axis=1, keepdims=True)
    slot_ids = iota((SLOTS, ROWS), 0)
    lane = iota((CLUSTERS, SLOTS), 1)
    lane_cluster, lane_rank = lax.div(lane, CAP), lax.rem(lane, CAP)

    def pack(k, owner, rows_ref, flag_ref):
        here = slot == (slot_ids + owner * SLOTS).astype(F32)
        rows_ref[k] = jnp.dot(
            here.astype(F32).astype(BF16), points[...], preferred_element_type=F32
        ).astype(BF16)
        mine = iota((CLUSTERS, SLOTS), 0) == lane_cluster + owner * PER_GROUP
        held = jnp.sum(jnp.where(mine, count, 0.0), axis=0, keepdims=True)
        live = (lane_rank[0:1].astype(F32) < held).astype(F32)
        flag_ref[k] = jnp.broadcast_to(live, (8, SLOTS))

    def row_copy(k):
        return remote(tx.at[k], rx.at[k], row_send.at[k], row_recv.at[k], (group_at(k), d))

    def flag_copy(k):
        return remote(txf.at[k], rxf.at[k], flag_send.at[k], flag_recv.at[k], (group_at(k), d))

    def aff_copy(k):
        return remote(afftx.at[k], affrx.at[k], aff_send.at[k], aff_recv.at[k], (group_from(k), d))

    def columns(axis):
        return pl.ds(axis * HALF, HALF)

    def gather1(axis, k):
        first, second = place[axis]
        piece = pool.at[d, :, columns(axis)]
        return remote(
            piece,
            piece,
            ag1_send.at[axis, k],
            ag1_recv.at[axis, k],
            (g, member(turn(first, k), second, axis)),
        )

    def gather2(axis, k1, k2):
        first, second = place[axis]
        piece = pool.at[member(turn(first, -k1), second, axis), :, columns(axis)]
        return remote(
            piece,
            piece,
            ag2_send.at[axis, k1, k2],
            ag2_recv.at[axis, k1, k2],
            (g, member(first, turn(second, k2), axis)),
        )

    points_in.wait()
    for k in ORDER[:2]:
        pack(k, group_at(k), tx, txf)
    cent_in.wait()
    pl.semaphore_wait(barrier, GROUPS - 1 + 6)
    for axis in (0, 1):
        for k in (2, 1, 3):
            gather1(axis, k).start()
    for i, k in enumerate(ORDER):
        if i >= 2:
            pack(k, group_at(k), tx, txf)
        row_copy(k).start()
        flag_copy(k).start()
        if i == 1:
            for axis in (0, 1):
                for k2 in (2, 1, 3):
                    gather2(axis, 0, k2).start()
    pack(0, g, rx, rxf)

    for k1 in (1, 3, 2):
        for axis in (0, 1):
            gather1(axis, k1).wait_recv()
            for k2 in (2, 1, 3):
                gather2(axis, k1, k2).start()

    cand_in.wait()
    block = iota((8, SLOTS), 0)
    allowed = jnp.zeros((8, SLOTS), jnp.bool_)
    wide_cluster = lax.div(iota((8, SLOTS), 1), CAP)
    for cluster in range(PER_GROUP):
        for j in range(LISTED):
            listed = cand[j, g * PER_GROUP + cluster]
            allowed = allowed | ((block == listed) & (wide_cluster == cluster))
    penalty = jnp.where(allowed, 0.0, FAR)

    for axis in (0, 1):
        for k1 in range(4):
            for k2 in range(1, 4):
                gather2(axis, k1, k2).wait_recv()

    for b in range(8):
        rows = pool[2 * b : 2 * b + 2].reshape(BLK, WIDTH).astype(F32)
        square = jnp.sum(rows * rows, axis=1, keepdims=True)
        norms[b] = square + penalty[b : b + 1]

    def score(number, pair):
        for k in pair:
            if k:
                row_copy(k).wait_recv()
                flag_copy(k).wait_recv()
        rows = jnp.concatenate([rx[k] for k in pair], axis=0)
        live = jnp.concatenate([rxf[k, 0:1] for k in pair], axis=1)

        def first(t, top):
            tile = pool[pl.ds(4 * t, 4)].reshape(4 * SHARD, WIDTH)
            inner = lax.dot_general(
                tile, rows, (((1,), (1,)), ((), ())), preferred_element_type=F32
            )
            square = norms[pl.ds(2 * t, 2)].reshape(4 * SHARD, SLOTS)
            value = (2.0 * inner - jnp.concatenate([square, square], axis=1)) * (
                1.0 / SOFTMAX_TEMP
            )
            logits[t] = value
            return jnp.maximum(top, jnp.max(value, axis=0, keepdims=True))

        top = lax.fori_loop(0, 4, first, jnp.full((1, 2 * SLOTS), -jnp.inf, F32))

        def second(t, total):
            value = jnp.exp(logits[t] - top)
            logits[t] = value
            return total + jnp.sum(value, axis=0, keepdims=True)

        total = lax.fori_loop(0, 4, second, jnp.zeros((1, 2 * SLOTS), F32))
        scale = live / total

        def third(t, carry):
            value = (logits[t] * scale).astype(BF16).reshape(4, SHARD, 2 * SLOTS)
            for i, k in enumerate(pair):
                weights[pl.ds(4 * t, 4), :, k * SLOTS : (k + 1) * SLOTS] = value[
                    :, :, i * SLOTS : (i + 1) * SLOTS
                ]
            return carry

        lax.fori_loop(0, 4, third, 0)
        affinity = SOFTMAX_TEMP * (top + jnp.log(total))
        for i, k in enumerate(pair):
            mine = jnp.broadcast_to(affinity[:, i * SLOTS : (i + 1) * SLOTS], (8, SLOTS))
            if k:
                afftx[k] = mine
                aff_copy(k).start()
            else:
                affrx[0] = mine

    for number, pair in enumerate(PAIRS):
        score(number, pair)

    part = (part_a, part_b)
    own = (own_a, own_b)
    far_in, near_in = (far_a, far_b), (near_a, near_b)
    send, last = (send_a, send_b), (last_a, last_b)

    def product(axis, index):
        if axis == 0:
            lhs = weights[pl.ds(4 * index, 4)].reshape(4 * SHARD, POOL)
        else:
            lhs = jnp.concatenate([weights[4 * i + index] for i in range(4)], axis=0)
        rhs = rx[:, :, axis * HALF : (axis + 1) * HALF].reshape(GROUPS * SLOTS, HALF)
        return jnp.dot(lhs, rhs, preferred_element_type=F32).reshape(4, SHARD, HALF)

    def share(sub):
        return pl.ds(sub * SUB, SUB)

    def hop(axis, sub, side, near, piece):
        first, second = place[axis]
        step = 1 - 2 * side
        span = pl.ds(piece * QUARTER, QUARTER)
        source = part[axis].at[turn(first, step if near else 2), :, share(sub), span]
        target = (g, member(turn(first, step), second, axis))
        if near:
            return remote(
                source,
                near_in[axis].at[side, :, share(sub), span],
                near_send.at[axis, sub, side, piece],
                near_recv.at[axis, sub, side, piece],
                target,
            )
        return remote(
            source,
            far_in[axis].at[side, :, share(sub)],
            far_send.at[axis, sub, side],
            far_recv.at[axis, sub, side],
            target,
        )

    def final(axis, sub, k):
        first, second = place[axis]
        return remote(
            send[axis].at[turn(second, k), share(sub)],
            last[axis].at[k - 1, share(sub)],
            last_send.at[axis, sub, k],
            last_recv.at[axis, sub, k],
            (g, member(first, turn(second, k), axis)),
        )

    for axis in (0, 1):
        index = turn(place[axis][0], 2)
        part[axis][index] = product(axis, index).astype(BF16)
        for side in (0, 1):
            hop(axis, 0, side, False, side).start()
    for axis in (0, 1):
        for side in (0, 1):
            index = turn(place[axis][0], 1 - 2 * side)
            part[axis][index] = product(axis, index).astype(BF16)
            hop(axis, 0, side, True, 1 - side).start()
        for side in (0, 1):
            hop(axis, 1, side, False, side).start()
    for axis in (0, 1):
        own[axis][...] = product(axis, place[axis][0])

    def relay(axis, sub, side):
        index = turn(place[axis][0], 1 - 2 * side)
        hop(axis, sub, side, False, side).wait_recv()
        rows = slice(sub * SUB, (sub + 1) * SUB)
        span = slice(side * QUARTER, (side + 1) * QUARTER)
        part[axis][index, :, rows, span] = (
            part[axis][index, :, rows, span].astype(F32) + far_in[axis][side, :, rows].astype(F32)
        ).astype(BF16)
        hop(axis, sub, side, True, side).start()

    for axis in (0, 1):
        for side in (0, 1):
            relay(axis, 0, side)
    for axis in (0, 1):
        for side in (0, 1):
            hop(axis, 1, side, True, 1 - side).start()

    lanes = iota((SHARD, BLK), 1)
    diagonal = lanes == iota((SHARD, BLK), 0)

    def total1(k):
        to = turn(z, k)
        return remote(tot1.at[to], tot1rx.at[k], tot_send.at[0, k], tot_recv.at[0, k], (g, to * 4 + y))

    def total2(k):
        to = turn(y, k)
        return remote(tot2.at[to], tot2rx.at[k], tot_send.at[1, k], tot_recv.at[1, k], (g, z * 4 + to))

    def total_of(i, carry):
        for j in range(4):
            column = jnp.sum(weights[4 * i + j].astype(F32), axis=1, keepdims=True)
            row = jnp.sum(jnp.where(diagonal, column, 0.0), axis=0, keepdims=True)
            tot1[i, j] = jnp.broadcast_to(row, (8, BLK))
        return carry

    lax.fori_loop(0, 4, total_of, 0)
    for k in range(1, 4):
        total1(k).start()

    for axis in (0, 1):
        for side in (0, 1):
            relay(axis, 1, side)

    totals = tot1[z]
    for k in range(1, 4):
        total1(k).wait_recv()
        totals = totals + tot1rx[k]
    tot2[...] = totals
    for k in range(1, 4):
        total2(k).start()

    affinity = jnp.zeros((1, ROWS), F32)
    square_eye = iota((SLOTS, SLOTS), 0) == iota((SLOTS, SLOTS), 1)
    for k in range(GROUPS):
        if k:
            aff_copy(k).wait_recv()
        column = jnp.sum(jnp.where(square_eye, affrx[k, 0:1], 0.0), axis=1, keepdims=True)
        here = slot == (slot_ids + group_at(k) * SLOTS).astype(F32)
        affinity = affinity + jnp.sum(jnp.where(here, column, 0.0), axis=0, keepdims=True)
    aff_ref[...] = affinity

    for sub in range(SUBS):
        rows = slice(sub * SUB, (sub + 1) * SUB)
        for axis in (0, 1):
            total = own[axis][:, rows]
            for side in (0, 1):
                for piece in (0, 1):
                    hop(axis, sub, side, True, piece).wait_recv()
                total = total + near_in[axis][side, :, rows].astype(F32)
            own[axis][:, rows] = total
            send[axis][:, rows] = total.astype(BF16)
            for k in (2, 1, 3):
                final(axis, sub, k).start()

    totals = tot2[y]
    for k in range(1, 4):
        total2(k).wait_recv()
        totals = totals + tot2rx[k]
    column = jnp.sum(jnp.where(diagonal, totals[0:1], 0.0), axis=1, keepdims=True) + PRIOR_WEIGHT

    for sub in range(SUBS):
        rows = slice(sub * SUB, (sub + 1) * SUB)
        for axis in (0, 1):
            total = own[axis][place[axis][1], rows]
            for k in range(1, 4):
                final(axis, sub, k).wait_recv()
                total = total + last[axis][k - 1, rows].astype(F32)
            span = slice(axis * HALF, (axis + 1) * HALF)
            prior = pool[d, rows, span].astype(F32)
            new_ref[rows, span] = (total + PRIOR_WEIGHT * prior) / column[rows]

    for k in range(1, GROUPS):
        flag_copy(k).wait_send()
        row_copy(k).wait_send()
        aff_copy(k).wait_send()
    for k in range(1, 4):
        total1(k).wait_send()
        total2(k).wait_send()
        for axis in (0, 1):
            gather1(axis, k).wait_send()
            for k1 in range(4):
                gather2(axis, k1, k).wait_send()
            for sub in range(SUBS):
                final(axis, sub, k).wait_send()
    for axis in (0, 1):
        for sub in range(SUBS):
            for side in (0, 1):
                hop(axis, sub, side, False, side).wait_send()
                for piece in (0, 1):
                    hop(axis, sub, side, True, piece).wait_send()


def local(points, coarse, candidates, centroids):
    vmem = pl.BlockSpec(memory_space=pltpu.VMEM)
    anywhere = pl.BlockSpec(memory_space=pl.ANY)
    dma = pltpu.SemaphoreType.DMA
    updated, affinity = pl.pallas_call(
        kernel,
        out_shape=(
            jax.ShapeDtypeStruct((SHARD, WIDTH), F32),
            jax.ShapeDtypeStruct((1, ROWS), F32),
        ),
        in_specs=[anywhere] * 4,
        out_specs=(vmem, vmem),
        scratch_shapes=[
            pltpu.SMEM((LISTED, CLUSTERS), jnp.int32),
            pltpu.VMEM((ROWS, WIDTH), BF16),
            pltpu.VMEM((1, ROWS), jnp.int32),
            pltpu.VMEM((GROUPS, SLOTS, WIDTH), BF16),
            pltpu.VMEM((GROUPS, SLOTS, WIDTH), BF16),
            pltpu.VMEM((GROUPS, 8, SLOTS), F32),
            pltpu.VMEM((GROUPS, 8, SLOTS), F32),
            pltpu.VMEM((MEMBERS, SHARD, WIDTH), BF16),
            pltpu.VMEM((8, BLK, SLOTS), F32),
            pltpu.VMEM((4, 4 * SHARD, 2 * SLOTS), F32),
            pltpu.VMEM((MEMBERS, SHARD, GROUPS * SLOTS), BF16),
            pltpu.VMEM((GROUPS, 8, SLOTS), F32),
            pltpu.VMEM((GROUPS, 8, SLOTS), F32),
            pltpu.VMEM((4, 4, 8, BLK), F32),
            pltpu.VMEM((4, 4, 8, BLK), F32),
            pltpu.VMEM((4, 8, BLK), F32),
            pltpu.VMEM((4, 8, BLK), F32),
            pltpu.VMEM((4, 4, SHARD, HALF), BF16),
            pltpu.VMEM((4, 4, SHARD, HALF), BF16),
            pltpu.VMEM((4, SHARD, HALF), F32),
            pltpu.VMEM((4, SHARD, HALF), F32),
            pltpu.VMEM((2, 4, SHARD, QUARTER), BF16),
            pltpu.VMEM((2, 4, SHARD, QUARTER), BF16),
            pltpu.VMEM((2, 4, SHARD, HALF), BF16),
            pltpu.VMEM((2, 4, SHARD, HALF), BF16),
            pltpu.VMEM((4, SHARD, HALF), BF16),
            pltpu.VMEM((4, SHARD, HALF), BF16),
            pltpu.VMEM((3, SHARD, HALF), BF16),
            pltpu.VMEM((3, SHARD, HALF), BF16),
            dma((4,)),
            dma((GROUPS,)),
            dma((GROUPS,)),
            dma((GROUPS,)),
            dma((GROUPS,)),
            dma((GROUPS,)),
            dma((GROUPS,)),
            dma((2, 4)),
            dma((2, 4)),
            dma((2, 4)),
            dma((2, 4)),
            dma((2, 4, 4)),
            dma((2, 4, 4)),
            dma((2, SUBS, 2)),
            dma((2, SUBS, 2)),
            dma((2, SUBS, 2, 2)),
            dma((2, SUBS, 2, 2)),
            dma((2, SUBS, 4)),
            dma((2, SUBS, 4)),
        ],
        compiler_params=pltpu.CompilerParams(
            collective_id=0, has_side_effects=True, vmem_limit_bytes=56 << 20
        ),
    )(candidates.T, points, coarse.reshape(1, ROWS), centroids)
    return updated, affinity.reshape(ROWS)


def solution(mesh):
    return jax.shard_map(
        local,
        mesh=mesh,
        in_specs=(P(("grp", "dev"), None), P(("grp", "dev"), None), P(), P(("grp", "dev"), None)),
        out_specs=(P(("grp", "dev"), None), P(("grp", "dev"))),
        check_vma=False,
    )
```

time: 65.5 us -> 56.9 us (0.87)
  the two profiles are of different devices: /device:TPU:0 before, /device:TPU:1 now
where the time goes in v2:
time: 56.9 us; the launch traced here: 56.4 us
  Pallas kernels  53.5 us (94%)
  local copies, waits for them, and re-layouts  2.25 us (4%)
  between operations  0.65 us (1%)
    pallas_call x1, Pallas kernels, local(): pl.pallas_call(kernel, out_shape=(jax.ShapeDtypeStruct((SHARD, WIDTH), F3...  53.5 us
    unnamed x4, local copies, waits for them, and re-layouts  2.25 us

profile of v2, /device:TPU:1, one launch (start us, length us, event | category | flops | bytes accessed | tf_op | source)
XLA Modules:
  0.0 56.4 jit_solution(13657821118251029106)
XLA Ops:
  0.6 53.5 %shard_map.59 = (f32[64,1024]{1,0:T(8,128)}, f32[1,512]{1,0:T(1,128)}) custom-call(s32[4,32]{1,0:T(4,128)} %bitcast.3, bf16[512,1024]{1,0:T(8,128)(2,1)} %points_hbm.1, s32[1,512]{1,0:T(1,128)} %bitcast.4, bf16[64,1024]{1,0:T(8,128)(2,1)} %cent_hbm.1), custom_call_target="tpu_custom_call" | custom-call | tf_op jit(solution)/shard_map/pallas_call | solution.py:477
  54.1 0.0 copy-start
  54.1 1.7 %copy.8 = f32[64,1024]{1,0:T(8,128)} copy(f32[64,1024]{1,0:T(8,128)} %get-tuple-element.8) | data formatting | bytes 524288
  55.8 0.0 copy-done
  55.8 0.6 %copy.9 = f32[512]{0:T(512)} copy(f32[512]{0:T(512)S(1)} %bitcast.5) | data formatting | bytes 4096
Async XLA Ops:
  54.1 1.7 %copy-start = (f32[1,512]{1,0:T(1,128)S(1)}, f32[1,512]{1,0:T(1,128)}, u32[]{:S(2)}) copy-start(f32[1,512]{1,0:T(1,128)} %get-tuple-element.5) | copy-start | bytes 6148

commit v3 on v2

--- a/solution.py
+++ b/solution.py
@@ -29,8 +29,8 @@
 QUARTER = WIDTH // 4
 SUBS = 2
 SUB = SHARD // SUBS
-ORDER = (4, 5, 2, 6, 3, 7, 1)
-PAIRS = ((0, 1), (4, 5), (2, 6), (3, 7))
+ORDER = (2, 6, 3, 7, 4, 5, 1)
+BATCHES = ((0, 1), (2, 6), (3, 7), (4,), (5,))
 
 
 def iota(shape, axis):
@@ -252,37 +252,30 @@
         rows = jnp.concatenate([rx[k] for k in pair], axis=0)
         live = jnp.concatenate([rxf[k, 0:1] for k in pair], axis=1)
 
-        def first(t, top):
-            tile = pool[pl.ds(4 * t, 4)].reshape(4 * SHARD, WIDTH)
+        wide = len(pair) * SLOTS
+        top = jnp.full((1, wide), -jnp.inf, F32)
+        for t in range(4):
+            tile = pool[4 * t : 4 * t + 4].reshape(4 * SHARD, WIDTH)
             inner = lax.dot_general(
                 tile, rows, (((1,), (1,)), ((), ())), preferred_element_type=F32
             )
-            square = norms[pl.ds(2 * t, 2)].reshape(4 * SHARD, SLOTS)
-            value = (2.0 * inner - jnp.concatenate([square, square], axis=1)) * (
-                1.0 / SOFTMAX_TEMP
-            )
-            logits[t] = value
-            return jnp.maximum(top, jnp.max(value, axis=0, keepdims=True))
-
-        top = lax.fori_loop(0, 4, first, jnp.full((1, 2 * SLOTS), -jnp.inf, F32))
-
-        def second(t, total):
-            value = jnp.exp(logits[t] - top)
-            logits[t] = value
-            return total + jnp.sum(value, axis=0, keepdims=True)
-
-        total = lax.fori_loop(0, 4, second, jnp.zeros((1, 2 * SLOTS), F32))
+            square = norms[2 * t : 2 * t + 2].reshape(4 * SHARD, SLOTS)
+            square = jnp.concatenate([square] * len(pair), axis=1)
+            value = (2.0 * inner - square) * (1.0 / SOFTMAX_TEMP)
+            logits[t, :, :wide] = value
+            top = jnp.maximum(top, jnp.max(value, axis=0, keepdims=True))
+        total = jnp.zeros((1, wide), F32)
+        for t in range(4):
+            value = jnp.exp(logits[t, :, :wide] - top)
+            logits[t, :, :wide] = value
+            total = total + jnp.sum(value, axis=0, keepdims=True)
         scale = live / total
-
-        def third(t, carry):
-            value = (logits[t] * scale).astype(BF16).reshape(4, SHARD, 2 * SLOTS)
+        for t in range(4):
+            value = (logits[t, :, :wide] * scale).astype(BF16).reshape(4, SHARD, wide)
             for i, k in enumerate(pair):
-                weights[pl.ds(4 * t, 4), :, k * SLOTS : (k + 1) * SLOTS] = value[
+                weights[4 * t : 4 * t + 4, :, k * SLOTS : (k + 1) * SLOTS] = value[
                     :, :, i * SLOTS : (i + 1) * SLOTS
                 ]
-            return carry
-
-        lax.fori_loop(0, 4, third, 0)
         affinity = SOFTMAX_TEMP * (top + jnp.log(total))
         for i, k in enumerate(pair):
             mine = jnp.broadcast_to(affinity[:, i * SLOTS : (i + 1) * SLOTS], (8, SLOTS))
@@ -292,7 +285,7 @@
             else:
                 affrx[0] = mine
 
-    for number, pair in enumerate(PAIRS):
+    for number, pair in enumerate(BATCHES):
         score(number, pair)
 
     part = (part_a, part_b)
@@ -417,7 +410,7 @@
         column = jnp.sum(jnp.where(square_eye, affrx[k, 0:1], 0.0), axis=1, keepdims=True)
         here = slot == (slot_ids + group_at(k) * SLOTS).astype(F32)
         affinity = affinity + jnp.sum(jnp.where(here, column, 0.0), axis=0, keepdims=True)
-    aff_ref[...] = affinity
+    aff_ref[...] = affinity.reshape(ROWS)
 
     for sub in range(SUBS):
         rows = slice(sub * SUB, (sub + 1) * SUB)
@@ -471,6 +464,7 @@
 
 
 def local(points, coarse, candidates, centroids):
+    operands = (candidates.T, points, coarse.reshape(1, ROWS), centroids)
     vmem = pl.BlockSpec(memory_space=pltpu.VMEM)
     anywhere = pl.BlockSpec(memory_space=pl.ANY)
     dma = pltpu.SemaphoreType.DMA
@@ -478,7 +472,7 @@
         kernel,
         out_shape=(
             jax.ShapeDtypeStruct((SHARD, WIDTH), F32),
-            jax.ShapeDtypeStruct((1, ROWS), F32),
+            jax.ShapeDtypeStruct((ROWS,), F32),
         ),
         in_specs=[anywhere] * 4,
         out_specs=(vmem, vmem),
@@ -533,10 +527,10 @@
             dma((2, SUBS, 4)),
         ],
         compiler_params=pltpu.CompilerParams(
-            collective_id=0, has_side_effects=True, vmem_limit_bytes=56 << 20
+            collective_id=0, has_side_effects=True, vmem_limit_bytes=32 << 20
         ),
-    )(candidates.T, points, coarse.reshape(1, ROWS), centroids)
-    return updated, affinity.reshape(ROWS)
+    )(*(pltpu.with_memory_space_constraint(a, pltpu.HBM) for a in operands))
+    return updated, affinity
 
 
 def solution(mesh):

time: 56.9 us -> 55.4 us (0.974)
  local copies, waits for them, and re-layouts: 2.25 us -> 1.28 us
    unnamed x4 -> x2, local copies, waits for them, and re-layouts: 2.25 us -> 1.28 us
where the time goes in v3:
time: 55.4 us; the launch traced here: 55.2 us
  Pallas kernels  53.3 us (96%)
  local copies, waits for them, and re-layouts  1.28 us (2%)
  between operations  0.64 us (1%)
    pallas_call x1, Pallas kernels, local(): pl.pallas_call(kernel, out_shape=(jax.ShapeDtypeStruct((SHARD, WIDTH), F3...  53.3 us
    unnamed x2, local copies, waits for them, and re-layouts  1.28 us

profile of v3, /device:TPU:1, one launch (start us, length us, event | category | flops | bytes accessed | tf_op | source)
XLA Modules:
  0.0 55.2 jit_solution(16693537676597824602)
XLA Ops:
  0.6 53.3 %shard_map.59 = (f32[64,1024]{1,0:T(8,128)S(1)}, f32[512]{0:T(512)S(1)}) custom-call(s32[4,32]{1,0:T(4,128)} %bitcast.2, bf16[512,1024]{1,0:T(8,128)(2,1)} %points_hbm.1, s32[1,512]{1,0:T(1,128)} %bitcast.3, bf16[64,1024]{1,0:T(8,128)(2,1)} %cent_hbm.1), custom_call_target="tpu_custom_call" | custom-call | tf_op jit(solution)/shard_map/pallas_call | solution.py:471
  53.9 0.7 %copy.8 = f32[64,1024]{1,0:T(8,128)} copy(f32[64,1024]{1,0:T(8,128)S(1)} %get-tuple-element.4) | data formatting | bytes 524288
  54.6 0.6 %copy.9 = f32[512]{0:T(512)} copy(f32[512]{0:T(512)S(1)} %get-tuple-element.5) | data formatting | bytes 4096

commit v4 on v3

--- a/solution.py
+++ b/solution.py
@@ -29,8 +29,9 @@
 QUARTER = WIDTH // 4
 SUBS = 2
 SUB = SHARD // SUBS
-ORDER = (2, 6, 3, 7, 4, 5, 1)
-BATCHES = ((0, 1), (2, 6), (3, 7), (4,), (5,))
+AWAY = ((0, 0), (0, 1), (1, 0), (3, 0), (1, 1), (3, 1), (2, 0), (2, 1))
+ORDER = (2, 3, 4, 5, 6, 7, 1)
+BATCHES = ((0, 1), (2, 3), (4, 5), (6,), (7,))
 
 
 def iota(shape, axis):
@@ -76,19 +77,14 @@
     in_sem,
     row_send,
     row_recv,
-    flag_send,
-    flag_recv,
-    aff_send,
-    aff_recv,
-    tot_send,
-    tot_recv,
-    ag1_send,
+    flag_sem,
+    aff_sem,
+    tot_sem,
+    ag_send,
     ag1_recv,
-    ag2_send,
     ag2_recv,
-    far_send,
+    part_send,
     far_recv,
-    near_send,
     near_recv,
     last_send,
     last_recv,
@@ -99,10 +95,10 @@
     z, y = lax.div(d, 4), lax.rem(d, 4)
 
     def group_at(k):
-        return lax.rem(x + k // 2, 4) * 2 + lax.rem(c + k % 2, 2)
+        return lax.rem(x + AWAY[k][0], 4) * 2 + lax.rem(c + AWAY[k][1], 2)
 
     def group_from(k):
-        return lax.rem(x + 4 - k // 2, 4) * 2 + lax.rem(c + k % 2, 2)
+        return lax.rem(x + 4 - AWAY[k][0], 4) * 2 + lax.rem(c + AWAY[k][1], 2)
 
     def turn(value, by):
         return lax.rem(value + by + 4, 4)
@@ -155,24 +151,33 @@
     lane = iota((CLUSTERS, SLOTS), 1)
     lane_cluster, lane_rank = lax.div(lane, CAP), lax.rem(lane, CAP)
 
-    def pack(k, owner, rows_ref, flag_ref):
-        here = slot == (slot_ids + owner * SLOTS).astype(F32)
-        rows_ref[k] = jnp.dot(
-            here.astype(F32).astype(BF16), points[...], preferred_element_type=F32
-        ).astype(BF16)
+    def flag(owner):
         mine = iota((CLUSTERS, SLOTS), 0) == lane_cluster + owner * PER_GROUP
         held = jnp.sum(jnp.where(mine, count, 0.0), axis=0, keepdims=True)
         live = (lane_rank[0:1].astype(F32) < held).astype(F32)
-        flag_ref[k] = jnp.broadcast_to(live, (8, SLOTS))
+        return jnp.broadcast_to(live, (8, SLOTS))
+
+    def pack(owner):
+        here = slot == (slot_ids + owner * SLOTS).astype(F32)
+        return jnp.dot(
+            here.astype(F32).astype(BF16), points[...], preferred_element_type=F32
+        ).astype(BF16)
 
     def row_copy(k):
-        return remote(tx.at[k], rx.at[k], row_send.at[k], row_recv.at[k], (group_at(k), d))
+        number = [k in batch for batch in BATCHES].index(True)
+        return remote(tx.at[k], rx.at[k], row_send, row_recv.at[number], (group_at(k), d))
 
     def flag_copy(k):
-        return remote(txf.at[k], rxf.at[k], flag_send.at[k], flag_recv.at[k], (group_at(k), d))
+        return remote(txf.at[k], rxf.at[k], flag_sem.at[0], flag_sem.at[1], (group_at(k), d))
 
     def aff_copy(k):
-        return remote(afftx.at[k], affrx.at[k], aff_send.at[k], aff_recv.at[k], (group_from(k), d))
+        return remote(afftx.at[k], affrx.at[k], aff_sem.at[0], aff_sem.at[1], (group_from(k), d))
+
+    def arrived(ref, sem):
+        remote(ref, ref, sem, sem, (g, d)).wait_recv()
+
+    def left(ref, sem):
+        remote(ref, ref, sem, sem, (g, d)).wait_send()
 
     def columns(axis):
         return pl.ds(axis * HALF, HALF)
@@ -183,8 +188,8 @@
         return remote(
             piece,
             piece,
-            ag1_send.at[axis, k],
-            ag1_recv.at[axis, k],
+            ag_send,
+            ag1_recv.at[axis, k - 1],
             (g, member(turn(first, k), second, axis)),
         )
 
@@ -194,29 +199,33 @@
         return remote(
             piece,
             piece,
-            ag2_send.at[axis, k1, k2],
-            ag2_recv.at[axis, k1, k2],
+            ag_send,
+            ag2_recv,
             (g, member(first, turn(second, k2), axis)),
         )
 
+    for k in ORDER:
+        txf[k] = flag(group_at(k))
+    rxf[0] = flag(g)
     points_in.wait()
     for k in ORDER[:2]:
-        pack(k, group_at(k), tx, txf)
+        tx[k] = pack(group_at(k))
     cent_in.wait()
     pl.semaphore_wait(barrier, GROUPS - 1 + 6)
     for axis in (0, 1):
         for k in (2, 1, 3):
             gather1(axis, k).start()
+    for k in ORDER:
+        flag_copy(k).start()
     for i, k in enumerate(ORDER):
         if i >= 2:
-            pack(k, group_at(k), tx, txf)
+            tx[k] = pack(group_at(k))
         row_copy(k).start()
-        flag_copy(k).start()
         if i == 1:
             for axis in (0, 1):
                 for k2 in (2, 1, 3):
                     gather2(axis, 0, k2).start()
-    pack(0, g, rx, rxf)
+    rx[0] = pack(g)
 
     for k1 in (1, 3, 2):
         for axis in (0, 1):
@@ -234,10 +243,8 @@
             allowed = allowed | ((block == listed) & (wide_cluster == cluster))
     penalty = jnp.where(allowed, 0.0, FAR)
 
-    for axis in (0, 1):
-        for k1 in range(4):
-            for k2 in range(1, 4):
-                gather2(axis, k1, k2).wait_recv()
+    arrived(pool.at[0:12], ag2_recv)
+    arrived(rxf.at[1:GROUPS], flag_sem.at[1])
 
     for b in range(8):
         rows = pool[2 * b : 2 * b + 2].reshape(BLK, WIDTH).astype(F32)
@@ -245,11 +252,9 @@
         norms[b] = square + penalty[b : b + 1]
 
     def score(number, pair):
-        for k in pair:
-            if k:
-                row_copy(k).wait_recv()
-                flag_copy(k).wait_recv()
-        rows = jnp.concatenate([rx[k] for k in pair], axis=0)
+        first = max(pair[0], 1)
+        arrived(rx.at[first : pair[-1] + 1], row_recv.at[number])
+        rows = rx[pair[0] : pair[-1] + 1].reshape(len(pair) * SLOTS, WIDTH)
         live = jnp.concatenate([rxf[k, 0:1] for k in pair], axis=1)
 
         wide = len(pair) * SLOTS
@@ -272,10 +277,7 @@
         scale = live / total
         for t in range(4):
             value = (logits[t, :, :wide] * scale).astype(BF16).reshape(4, SHARD, wide)
-            for i, k in enumerate(pair):
-                weights[4 * t : 4 * t + 4, :, k * SLOTS : (k + 1) * SLOTS] = value[
-                    :, :, i * SLOTS : (i + 1) * SLOTS
-                ]
+            weights[4 * t : 4 * t + 4, :, pair[0] * SLOTS : (pair[-1] + 1) * SLOTS] = value
         affinity = SOFTMAX_TEMP * (top + jnp.log(total))
         for i, k in enumerate(pair):
             mine = jnp.broadcast_to(affinity[:, i * SLOTS : (i + 1) * SLOTS], (8, SLOTS))
@@ -314,15 +316,15 @@
             return remote(
                 source,
                 near_in[axis].at[side, :, share(sub), span],
-                near_send.at[axis, sub, side, piece],
-                near_recv.at[axis, sub, side, piece],
+                part_send.at[axis],
+                near_recv.at[axis, sub],
                 target,
             )
         return remote(
             source,
             far_in[axis].at[side, :, share(sub)],
-            far_send.at[axis, sub, side],
-            far_recv.at[axis, sub, side],
+            part_send.at[axis],
+            far_recv.at[axis, sub],
             target,
         )
 
@@ -331,8 +333,8 @@
         return remote(
             send[axis].at[turn(second, k), share(sub)],
             last[axis].at[k - 1, share(sub)],
-            last_send.at[axis, sub, k],
-            last_recv.at[axis, sub, k],
+            last_send.at[axis],
+            last_recv.at[axis, sub],
             (g, member(first, turn(second, k), axis)),
         )
 
@@ -351,19 +353,20 @@
     for axis in (0, 1):
         own[axis][...] = product(axis, place[axis][0])
 
-    def relay(axis, sub, side):
-        index = turn(place[axis][0], 1 - 2 * side)
-        hop(axis, sub, side, False, side).wait_recv()
+    def relay(axis, sub):
         rows = slice(sub * SUB, (sub + 1) * SUB)
-        span = slice(side * QUARTER, (side + 1) * QUARTER)
-        part[axis][index, :, rows, span] = (
-            part[axis][index, :, rows, span].astype(F32) + far_in[axis][side, :, rows].astype(F32)
-        ).astype(BF16)
-        hop(axis, sub, side, True, side).start()
-
-    for axis in (0, 1):
+        arrived(far_in[axis].at[:, :, share(sub)], far_recv.at[axis, sub])
         for side in (0, 1):
-            relay(axis, 0, side)
+            index = turn(place[axis][0], 1 - 2 * side)
+            span = slice(side * QUARTER, (side + 1) * QUARTER)
+            part[axis][index, :, rows, span] = (
+                part[axis][index, :, rows, span].astype(F32)
+                + far_in[axis][side, :, rows].astype(F32)
+            ).astype(BF16)
+            hop(axis, sub, side, True, side).start()
+
+    for axis in (0, 1):
+        relay(axis, 0)
     for axis in (0, 1):
         for side in (0, 1):
             hop(axis, 1, side, True, 1 - side).start()
@@ -373,11 +376,11 @@
 
     def total1(k):
         to = turn(z, k)
-        return remote(tot1.at[to], tot1rx.at[k], tot_send.at[0, k], tot_recv.at[0, k], (g, to * 4 + y))
+        return remote(tot1.at[to], tot1rx.at[k], tot_sem.at[0], tot_sem.at[1], (g, to * 4 + y))
 
     def total2(k):
         to = turn(y, k)
-        return remote(tot2.at[to], tot2rx.at[k], tot_send.at[1, k], tot_recv.at[1, k], (g, z * 4 + to))
+        return remote(tot2.at[to], tot2rx.at[k], tot_sem.at[2], tot_sem.at[3], (g, z * 4 + to))
 
     def total_of(i, carry):
         for j in range(4):
@@ -391,12 +394,11 @@
         total1(k).start()
 
     for axis in (0, 1):
-        for side in (0, 1):
-            relay(axis, 1, side)
-
+        relay(axis, 1)
+
+    arrived(tot1rx.at[1:4], tot_sem.at[1])
     totals = tot1[z]
     for k in range(1, 4):
-        total1(k).wait_recv()
         totals = totals + tot1rx[k]
     tot2[...] = totals
     for k in range(1, 4):
@@ -404,9 +406,8 @@
 
     affinity = jnp.zeros((1, ROWS), F32)
     square_eye = iota((SLOTS, SLOTS), 0) == iota((SLOTS, SLOTS), 1)
+    arrived(affrx.at[1:GROUPS], aff_sem.at[1])
     for k in range(GROUPS):
-        if k:
-            aff_copy(k).wait_recv()
         column = jnp.sum(jnp.where(square_eye, affrx[k, 0:1], 0.0), axis=1, keepdims=True)
         here = slot == (slot_ids + group_at(k) * SLOTS).astype(F32)
         affinity = affinity + jnp.sum(jnp.where(here, column, 0.0), axis=0, keepdims=True)
@@ -416,9 +417,8 @@
         rows = slice(sub * SUB, (sub + 1) * SUB)
         for axis in (0, 1):
             total = own[axis][:, rows]
+            arrived(near_in[axis].at[:, :, share(sub)], near_recv.at[axis, sub])
             for side in (0, 1):
-                for piece in (0, 1):
-                    hop(axis, sub, side, True, piece).wait_recv()
                 total = total + near_in[axis][side, :, rows].astype(F32)
             own[axis][:, rows] = total
             send[axis][:, rows] = total.astype(BF16)
@@ -426,8 +426,8 @@
                 final(axis, sub, k).start()
 
     totals = tot2[y]
+    arrived(tot2rx.at[1:4], tot_sem.at[3])
     for k in range(1, 4):
-        total2(k).wait_recv()
         totals = totals + tot2rx[k]
     column = jnp.sum(jnp.where(diagonal, totals[0:1], 0.0), axis=1, keepdims=True) + PRIOR_WEIGHT
 
@@ -435,32 +435,22 @@
         rows = slice(sub * SUB, (sub + 1) * SUB)
         for axis in (0, 1):
             total = own[axis][place[axis][1], rows]
+            arrived(last[axis].at[:, share(sub)], last_recv.at[axis, sub])
             for k in range(1, 4):
-                final(axis, sub, k).wait_recv()
                 total = total + last[axis][k - 1, rows].astype(F32)
             span = slice(axis * HALF, (axis + 1) * HALF)
             prior = pool[d, rows, span].astype(F32)
             new_ref[rows, span] = (total + PRIOR_WEIGHT * prior) / column[rows]
 
-    for k in range(1, GROUPS):
-        flag_copy(k).wait_send()
-        row_copy(k).wait_send()
-        aff_copy(k).wait_send()
-    for k in range(1, 4):
-        total1(k).wait_send()
-        total2(k).wait_send()
-        for axis in (0, 1):
-            gather1(axis, k).wait_send()
-            for k1 in range(4):
-                gather2(axis, k1, k).wait_send()
-            for sub in range(SUBS):
-                final(axis, sub, k).wait_send()
-    for axis in (0, 1):
-        for sub in range(SUBS):
-            for side in (0, 1):
-                hop(axis, sub, side, False, side).wait_send()
-                for piece in (0, 1):
-                    hop(axis, sub, side, True, piece).wait_send()
+    left(tx.at[1:GROUPS], row_send)
+    left(txf.at[1:GROUPS], flag_sem.at[0])
+    left(afftx.at[1:GROUPS], aff_sem.at[0])
+    left(tot1.at[0:3], tot_sem.at[0])
+    left(tot2.at[0:3], tot_sem.at[2])
+    left(pool.at[0:15], ag_send)
+    for axis in (0, 1):
+        left(part[axis].at[0:3], part_send.at[axis])
+        left(last[axis], last_send.at[axis])
 
 
 def local(points, coarse, candidates, centroids):
@@ -507,24 +497,19 @@
             pltpu.VMEM((3, SHARD, HALF), BF16),
             pltpu.VMEM((3, SHARD, HALF), BF16),
             dma((4,)),
-            dma((GROUPS,)),
-            dma((GROUPS,)),
-            dma((GROUPS,)),
-            dma((GROUPS,)),
-            dma((GROUPS,)),
-            dma((GROUPS,)),
-            dma((2, 4)),
-            dma((2, 4)),
-            dma((2, 4)),
-            dma((2, 4)),
-            dma((2, 4, 4)),
-            dma((2, 4, 4)),
-            dma((2, SUBS, 2)),
-            dma((2, SUBS, 2)),
-            dma((2, SUBS, 2, 2)),
-            dma((2, SUBS, 2, 2)),
-            dma((2, SUBS, 4)),
-            dma((2, SUBS, 4)),
+            dma,
+            dma((len(BATCHES),)),
+            dma((2,)),
+            dma((2,)),
+            dma((4,)),
+            dma,
+            dma((2, 3)),
+            dma,
+            dma((2,)),
+            dma((2, SUBS)),
+            dma((2, SUBS)),
+            dma((2,)),
+            dma((2, SUBS)),
         ],
         compiler_params=pltpu.CompilerParams(
             collective_id=0, has_side_effects=True, vmem_limit_bytes=32 << 20

time: 55.4 us -> 52.9 us (0.955)
  Pallas kernels: 53.3 us -> 50.9 us
    pallas_call x1, Pallas kernels: 53.3 us -> 50.9 us  [local(): pl.pallas_call(kernel, out_shape=(jax.ShapeDtypeStruct((SHARD, WIDTH), F3...]
where the time goes in v4:
time: 52.9 us; the launch traced here: 52.8 us
  Pallas kernels  50.9 us (96%)
  local copies, waits for them, and re-layouts  1.28 us (2%)
  between operations  0.64 us (1%)
    pallas_call x1, Pallas kernels, local(): pl.pallas_call(kernel, out_shape=(jax.ShapeDtypeStruct((SHARD, WIDTH), F3...  50.9 us
    unnamed x2, local copies, waits for them, and re-layouts  1.28 us

profile of v4, /device:TPU:1, one launch (start us, length us, event | category | flops | bytes accessed | tf_op | source)
XLA Modules:
  0.0 52.8 jit_solution(3827339528375478340)
XLA Ops:
  0.6 50.9 %shard_map.59 = (f32[64,1024]{1,0:T(8,128)S(1)}, f32[512]{0:T(512)S(1)}) custom-call(s32[4,32]{1,0:T(4,128)} %bitcast.2, bf16[512,1024]{1,0:T(8,128)(2,1)} %points_hbm.1, s32[1,512]{1,0:T(1,128)} %bitcast.3, bf16[64,1024]{1,0:T(8,128)(2,1)} %cent_hbm.1), custom_call_target="tpu_custom_call" | custom-call | tf_op jit(solution)/shard_map/pallas_call | solution.py:461
  51.5 0.7 %copy.8 = f32[64,1024]{1,0:T(8,128)} copy(f32[64,1024]{1,0:T(8,128)S(1)} %get-tuple-element.4) | data formatting | bytes 524288
  52.2 0.6 %copy.9 = f32[512]{0:T(512)} copy(f32[512]{0:T(512)S(1)} %get-tuple-element.5) | data formatting | bytes 4096

commit v5 on v4

--- a/solution.py
+++ b/solution.py
@@ -27,8 +27,8 @@
 SLOTS = PER_GROUP * CAP
 HALF = WIDTH // 2
 QUARTER = WIDTH // 4
-SUBS = 2
-SUB = SHARD // SUBS
+SPANS = ((0, 1), (1, 2), (2, 4))
+SUBS = len(SPANS)
 AWAY = ((0, 0), (0, 1), (1, 0), (3, 0), (1, 1), (3, 1), (2, 0), (2, 1))
 ORDER = (2, 3, 4, 5, 6, 7, 1)
 BATCHES = ((0, 1), (2, 3), (4, 5), (6,), (7,))
@@ -208,20 +208,20 @@
         txf[k] = flag(group_at(k))
     rxf[0] = flag(g)
     points_in.wait()
-    for k in ORDER[:2]:
-        tx[k] = pack(group_at(k))
-    cent_in.wait()
+    tx[ORDER[0]] = pack(group_at(ORDER[0]))
     pl.semaphore_wait(barrier, GROUPS - 1 + 6)
-    for axis in (0, 1):
-        for k in (2, 1, 3):
-            gather1(axis, k).start()
-    for k in ORDER:
-        flag_copy(k).start()
     for i, k in enumerate(ORDER):
-        if i >= 2:
+        if i:
             tx[k] = pack(group_at(k))
         row_copy(k).start()
         if i == 1:
+            for k1 in ORDER:
+                flag_copy(k1).start()
+            cent_in.wait()
+            for axis in (0, 1):
+                for k1 in (2, 1, 3):
+                    gather1(axis, k1).start()
+        if i == 2:
             for axis in (0, 1):
                 for k2 in (2, 1, 3):
                     gather2(axis, 0, k2).start()
@@ -296,80 +296,79 @@
     send, last = (send_a, send_b), (last_a, last_b)
 
     def product(axis, index):
-        if axis == 0:
-            lhs = weights[pl.ds(4 * index, 4)].reshape(4 * SHARD, POOL)
-        else:
-            lhs = jnp.concatenate([weights[4 * i + index] for i in range(4)], axis=0)
+        lhs = jnp.concatenate([weights[member(index, i, axis)] for i in range(4)], axis=0)
         rhs = rx[:, :, axis * HALF : (axis + 1) * HALF].reshape(GROUPS * SLOTS, HALF)
         return jnp.dot(lhs, rhs, preferred_element_type=F32).reshape(4, SHARD, HALF)
 
-    def share(sub):
-        return pl.ds(sub * SUB, SUB)
+    def span_of(sub):
+        return pl.ds(SPANS[sub][0], SPANS[sub][1] - SPANS[sub][0])
 
     def hop(axis, sub, side, near, piece):
         first, second = place[axis]
         step = 1 - 2 * side
         span = pl.ds(piece * QUARTER, QUARTER)
-        source = part[axis].at[turn(first, step if near else 2), :, share(sub), span]
+        source = part[axis].at[turn(first, step if near else 2), span_of(sub), :, span]
         target = (g, member(turn(first, step), second, axis))
         if near:
-            return remote(
-                source,
-                near_in[axis].at[side, :, share(sub), span],
-                part_send.at[axis],
-                near_recv.at[axis, sub],
-                target,
-            )
-        return remote(
-            source,
-            far_in[axis].at[side, :, share(sub)],
-            part_send.at[axis],
-            far_recv.at[axis, sub],
-            target,
-        )
-
-    def final(axis, sub, k):
+            landing = near_in[axis].at[side, span_of(sub), :, span]
+            return remote(source, landing, part_send.at[axis], near_recv.at[axis, sub], target)
+        landing = far_in[axis].at[side, span_of(sub)]
+        return remote(source, landing, part_send.at[axis], far_recv.at[axis, sub], target)
+
+    def far(axis, sub):
+        for side in (0, 1):
+            hop(axis, sub, side, False, side).start()
+
+    def direct(axis, sub):
+        for side in (0, 1):
+            hop(axis, sub, side, True, 1 - side).start()
+
+    def relay(axis, sub):
+        low, high = SPANS[sub]
+        arrived(far_in[axis].at[:, span_of(sub)], far_recv.at[axis, sub])
+        for side in (0, 1):
+            index = turn(place[axis][0], 1 - 2 * side)
+            span = slice(side * QUARTER, (side + 1) * QUARTER)
+            part[axis][index, low:high, :, span] = (
+                part[axis][index, low:high, :, span].astype(F32)
+                + far_in[axis][side, low:high].astype(F32)
+            ).astype(BF16)
+            hop(axis, sub, side, True, side).start()
+
+    def final(axis, sub):
         first, second = place[axis]
-        return remote(
-            send[axis].at[turn(second, k), share(sub)],
-            last[axis].at[k - 1, share(sub)],
-            last_send.at[axis],
-            last_recv.at[axis, sub],
-            (g, member(first, turn(second, k), axis)),
-        )
+        low, high = SPANS[sub]
+        arrived(near_in[axis].at[:, span_of(sub)], near_recv.at[axis, sub])
+        total = own[axis][low:high]
+        for side in (0, 1):
+            total = total + near_in[axis][side, low:high].astype(F32)
+        own[axis][low:high] = total
+        send[axis][low:high] = total.astype(BF16)
+        for holder in range(low, high):
+
+            @pl.when(second != holder)
+            def _():
+                remote(
+                    send[axis].at[holder],
+                    last[axis].at[turn(second, -holder) - 1],
+                    last_send.at[axis],
+                    last_recv.at[axis],
+                    (g, member(first, holder, axis)),
+                ).start()
 
     for axis in (0, 1):
         index = turn(place[axis][0], 2)
         part[axis][index] = product(axis, index).astype(BF16)
-        for side in (0, 1):
-            hop(axis, 0, side, False, side).start()
+        for sub in range(SUBS):
+            far(axis, sub)
     for axis in (0, 1):
         for side in (0, 1):
             index = turn(place[axis][0], 1 - 2 * side)
             part[axis][index] = product(axis, index).astype(BF16)
-            hop(axis, 0, side, True, 1 - side).start()
-        for side in (0, 1):
-            hop(axis, 1, side, False, side).start()
+        for sub in range(SUBS):
+            direct(axis, sub)
     for axis in (0, 1):
         own[axis][...] = product(axis, place[axis][0])
-
-    def relay(axis, sub):
-        rows = slice(sub * SUB, (sub + 1) * SUB)
-        arrived(far_in[axis].at[:, :, share(sub)], far_recv.at[axis, sub])
-        for side in (0, 1):
-            index = turn(place[axis][0], 1 - 2 * side)
-            span = slice(side * QUARTER, (side + 1) * QUARTER)
-            part[axis][index, :, rows, span] = (
-                part[axis][index, :, rows, span].astype(F32)
-                + far_in[axis][side, :, rows].astype(F32)
-            ).astype(BF16)
-            hop(axis, sub, side, True, side).start()
-
-    for axis in (0, 1):
-        relay(axis, 0)
-    for axis in (0, 1):
-        for side in (0, 1):
-            hop(axis, 1, side, True, 1 - side).start()
 
     lanes = iota((SHARD, BLK), 1)
     diagonal = lanes == iota((SHARD, BLK), 0)
@@ -390,12 +389,17 @@
         return carry
 
     lax.fori_loop(0, 4, total_of, 0)
+
+    for axis in (0, 1):
+        relay(axis, 0)
+    for axis in (0, 1):
+        relay(axis, 1)
     for k in range(1, 4):
         total1(k).start()
-
-    for axis in (0, 1):
-        relay(axis, 1)
-
+    for axis in (0, 1):
+        relay(axis, 2)
+    for axis in (0, 1):
+        final(axis, 0)
     arrived(tot1rx.at[1:4], tot_sem.at[1])
     totals = tot1[z]
     for k in range(1, 4):
@@ -403,6 +407,10 @@
     tot2[...] = totals
     for k in range(1, 4):
         total2(k).start()
+    for axis in (0, 1):
+        final(axis, 1)
+    for axis in (0, 1):
+        final(axis, 2)
 
     affinity = jnp.zeros((1, ROWS), F32)
     square_eye = iota((SLOTS, SLOTS), 0) == iota((SLOTS, SLOTS), 1)
@@ -413,34 +421,21 @@
         affinity = affinity + jnp.sum(jnp.where(here, column, 0.0), axis=0, keepdims=True)
     aff_ref[...] = affinity.reshape(ROWS)
 
-    for sub in range(SUBS):
-        rows = slice(sub * SUB, (sub + 1) * SUB)
-        for axis in (0, 1):
-            total = own[axis][:, rows]
-            arrived(near_in[axis].at[:, :, share(sub)], near_recv.at[axis, sub])
-            for side in (0, 1):
-                total = total + near_in[axis][side, :, rows].astype(F32)
-            own[axis][:, rows] = total
-            send[axis][:, rows] = total.astype(BF16)
-            for k in (2, 1, 3):
-                final(axis, sub, k).start()
-
     totals = tot2[y]
     arrived(tot2rx.at[1:4], tot_sem.at[3])
     for k in range(1, 4):
         totals = totals + tot2rx[k]
     column = jnp.sum(jnp.where(diagonal, totals[0:1], 0.0), axis=1, keepdims=True) + PRIOR_WEIGHT
 
-    for sub in range(SUBS):
-        rows = slice(sub * SUB, (sub + 1) * SUB)
-        for axis in (0, 1):
-            total = own[axis][place[axis][1], rows]
-            arrived(last[axis].at[:, share(sub)], last_recv.at[axis, sub])
-            for k in range(1, 4):
-                total = total + last[axis][k - 1, rows].astype(F32)
-            span = slice(axis * HALF, (axis + 1) * HALF)
-            prior = pool[d, rows, span].astype(F32)
-            new_ref[rows, span] = (total + PRIOR_WEIGHT * prior) / column[rows]
+    for axis in (0, 1):
+        second = place[axis][1]
+        total = own[axis][second]
+        arrived(last[axis], last_recv.at[axis])
+        for k in range(3):
+            total = total + last[axis][k].astype(F32)
+        span = slice(axis * HALF, (axis + 1) * HALF)
+        prior = pool[d, :, span].astype(F32)
+        new_ref[:, span] = (total + PRIOR_WEIGHT * prior) / column
 
     left(tx.at[1:GROUPS], row_send)
     left(txf.at[1:GROUPS], flag_sem.at[0])
@@ -509,7 +504,7 @@
             dma((2, SUBS)),
             dma((2, SUBS)),
             dma((2,)),
-            dma((2, SUBS)),
+            dma((2,)),
         ],
         compiler_params=pltpu.CompilerParams(
             collective_id=0, has_side_effects=True, vmem_limit_bytes=32 << 20

time: 52.9 us -> 51.6 us (0.975)
  Pallas kernels: 50.9 us -> 49.6 us
    pallas_call x1, Pallas kernels: 50.9 us -> 49.6 us  [local(): pl.pallas_call(kernel, out_shape=(jax.ShapeDtypeStruct((SHARD, WIDTH), F3...]
where the time goes in v5:
time: 51.6 us; the launch traced here: 51.5 us
  Pallas kernels  49.6 us (96%)
  local copies, waits for them, and re-layouts  1.28 us (2%)
  between operations  0.64 us (1%)
    pallas_call x1, Pallas kernels, local(): pl.pallas_call(kernel, out_shape=(jax.ShapeDtypeStruct((SHARD, WIDTH), F3...  49.6 us
    unnamed x2, local copies, waits for them, and re-layouts  1.28 us

profile of v5, /device:TPU:1, one launch (start us, length us, event | category | flops | bytes accessed | tf_op | source)
XLA Modules:
  0.0 51.5 jit_solution(10306448530731912570)
XLA Ops:
  0.6 49.6 %shard_map.59 = (f32[64,1024]{1,0:T(8,128)S(1)}, f32[512]{0:T(512)S(1)}) custom-call(s32[4,32]{1,0:T(4,128)} %bitcast.2, bf16[512,1024]{1,0:T(8,128)(2,1)} %points_hbm.1, s32[1,512]{1,0:T(1,128)} %bitcast.3, bf16[64,1024]{1,0:T(8,128)(2,1)} %cent_hbm.1), custom_call_target="tpu_custom_call" | custom-call | tf_op jit(solution)/shard_map/pallas_call | solution.py:456
  50.2 0.7 %copy.8 = f32[64,1024]{1,0:T(8,128)} copy(f32[64,1024]{1,0:T(8,128)S(1)} %get-tuple-element.4) | data formatting | bytes 524288
  50.9 0.6 %copy.9 = f32[512]{0:T(512)} copy(f32[512]{0:T(512)S(1)} %get-tuple-element.5) | data formatting | bytes 4096

commit v6 on v5

--- a/solution.py
+++ b/solution.py
@@ -29,9 +29,11 @@
 QUARTER = WIDTH // 4
 SPANS = ((0, 1), (1, 2), (2, 4))
 SUBS = len(SPANS)
+EARLY = 6
 AWAY = ((0, 0), (0, 1), (1, 0), (3, 0), (1, 1), (3, 1), (2, 0), (2, 1))
 ORDER = (2, 3, 4, 5, 6, 7, 1)
 BATCHES = ((0, 1), (2, 3), (4, 5), (6,), (7,))
+LAST = GROUPS - 1
 
 
 def iota(shape, axis):
@@ -64,6 +66,9 @@
     tot2rx,
     part_a,
     part_b,
+    acc_a,
+    acc_b,
+    early,
     own_a,
     own_b,
     far_a,
@@ -163,10 +168,23 @@
             here.astype(F32).astype(BF16), points[...], preferred_element_type=F32
         ).astype(BF16)
 
+    def columns(axis):
+        return pl.ds(axis * HALF, HALF)
+
     def row_copy(k):
         number = [k in batch for batch in BATCHES].index(True)
         return remote(tx.at[k], rx.at[k], row_send, row_recv.at[number], (group_at(k), d))
 
+    def last_row_copy(half):
+        span = columns(half)
+        return remote(
+            tx.at[LAST, :, span],
+            rx.at[LAST, :, span],
+            row_send,
+            row_recv.at[len(BATCHES) - 1 + half],
+            (group_at(LAST), d),
+        )
+
     def flag_copy(k):
         return remote(txf.at[k], rxf.at[k], flag_sem.at[0], flag_sem.at[1], (group_at(k), d))
 
@@ -178,9 +196,6 @@
 
     def left(ref, sem):
         remote(ref, ref, sem, sem, (g, d)).wait_send()
-
-    def columns(axis):
-        return pl.ds(axis * HALF, HALF)
 
     def gather1(axis, k):
         first, second = place[axis]
@@ -213,7 +228,11 @@
     for i, k in enumerate(ORDER):
         if i:
             tx[k] = pack(group_at(k))
-        row_copy(k).start()
+        if k == LAST:
+            last_row_copy(0).start()
+            last_row_copy(1).start()
+        else:
+            row_copy(k).start()
         if i == 1:
             for k1 in ORDER:
                 flag_copy(k1).start()
@@ -252,18 +271,33 @@
         norms[b] = square + penalty[b : b + 1]
 
     def score(number, pair):
-        first = max(pair[0], 1)
-        arrived(rx.at[first : pair[-1] + 1], row_recv.at[number])
-        rows = rx[pair[0] : pair[-1] + 1].reshape(len(pair) * SLOTS, WIDTH)
+        if pair[0] == LAST:
+            arrived(rx.at[LAST, :, columns(0)], row_recv.at[number])
+        else:
+            first = max(pair[0], 1)
+            arrived(rx.at[first : pair[-1] + 1], row_recv.at[number])
         live = jnp.concatenate([rxf[k, 0:1] for k in pair], axis=1)
 
         wide = len(pair) * SLOTS
+
+        def inner_products(t, span):
+            return lax.dot_general(
+                pool[4 * t : 4 * t + 4, :, span].reshape(4 * SHARD, -1),
+                rx[pair[0] : pair[-1] + 1, :, span].reshape(wide, -1),
+                (((1,), (1,)), ((), ())),
+                preferred_element_type=F32,
+            )
+
+        if pair[0] == LAST:
+            for t in range(4):
+                logits[t, :, :wide] = inner_products(t, slice(0, HALF))
+            arrived(rx.at[LAST, :, columns(1)], row_recv.at[number + 1])
         top = jnp.full((1, wide), -jnp.inf, F32)
         for t in range(4):
-            tile = pool[4 * t : 4 * t + 4].reshape(4 * SHARD, WIDTH)
-            inner = lax.dot_general(
-                tile, rows, (((1,), (1,)), ((), ())), preferred_element_type=F32
-            )
+            if pair[0] == LAST:
+                inner = logits[t, :, :wide] + inner_products(t, slice(HALF, WIDTH))
+            else:
+                inner = inner_products(t, slice(0, WIDTH))
             square = norms[2 * t : 2 * t + 2].reshape(4 * SHARD, SLOTS)
             square = jnp.concatenate([square] * len(pair), axis=1)
             value = (2.0 * inner - square) * (1.0 / SOFTMAX_TEMP)
@@ -287,18 +321,39 @@
             else:
                 affrx[0] = mine
 
+    acc = (acc_a, acc_b)
+
+    def partial(axis, index, low, high):
+        lanes = slice(low * SLOTS, high * SLOTS)
+        lhs = jnp.concatenate([weights[member(index, i, axis), :, lanes] for i in range(4)], axis=0)
+        rhs = rx[low:high, :, axis * HALF : (axis + 1) * HALF].reshape((high - low) * SLOTS, HALF)
+        return jnp.dot(lhs, rhs, preferred_element_type=F32).reshape(4, SHARD, HALF)
+
+    def product(axis, index):
+        return acc[axis][index] + partial(axis, index, EARLY, GROUPS)
+
+    def lane_sums(i, low, high):
+        total = weights[i, :, low * SLOTS : (low + 1) * SLOTS].astype(F32)
+        for k in range(low + 1, high):
+            total = total + weights[i, :, k * SLOTS : (k + 1) * SLOTS].astype(F32)
+        return total
+
+    def early_sums(i, carry):
+        early[i] = lane_sums(i, 0, EARLY)
+        return carry
+
     for number, pair in enumerate(BATCHES):
+        if pair[0] == EARLY:
+            for axis in (0, 1):
+                for index in range(4):
+                    acc[axis][index] = partial(axis, index, 0, EARLY)
+            lax.fori_loop(0, MEMBERS, early_sums, 0)
         score(number, pair)
 
     part = (part_a, part_b)
     own = (own_a, own_b)
     far_in, near_in = (far_a, far_b), (near_a, near_b)
     send, last = (send_a, send_b), (last_a, last_b)
-
-    def product(axis, index):
-        lhs = jnp.concatenate([weights[member(index, i, axis)] for i in range(4)], axis=0)
-        rhs = rx[:, :, axis * HALF : (axis + 1) * HALF].reshape(GROUPS * SLOTS, HALF)
-        return jnp.dot(lhs, rhs, preferred_element_type=F32).reshape(4, SHARD, HALF)
 
     def span_of(sub):
         return pl.ds(SPANS[sub][0], SPANS[sub][1] - SPANS[sub][0])
@@ -383,7 +438,8 @@
 
     def total_of(i, carry):
         for j in range(4):
-            column = jnp.sum(weights[4 * i + j].astype(F32), axis=1, keepdims=True)
+            found = early[4 * i + j] + lane_sums(4 * i + j, EARLY, GROUPS)
+            column = jnp.sum(found, axis=1, keepdims=True)
             row = jnp.sum(jnp.where(diagonal, column, 0.0), axis=0, keepdims=True)
             tot1[i, j] = jnp.broadcast_to(row, (8, BLK))
         return carry
@@ -481,6 +537,9 @@
             pltpu.VMEM((4, 8, BLK), F32),
             pltpu.VMEM((4, 4, SHARD, HALF), BF16),
             pltpu.VMEM((4, 4, SHARD, HALF), BF16),
+            pltpu.VMEM((4, 4, SHARD, HALF), F32),
+            pltpu.VMEM((4, 4, SHARD, HALF), F32),
+            pltpu.VMEM((MEMBERS, SHARD, BLK), F32),
             pltpu.VMEM((4, SHARD, HALF), F32),
             pltpu.VMEM((4, SHARD, HALF), F32),
             pltpu.VMEM((2, 4, SHARD, QUARTER), BF16),
@@ -493,7 +552,7 @@
             pltpu.VMEM((3, SHARD, HALF), BF16),
             dma((4,)),
             dma,
-            dma((len(BATCHES),)),
+            dma((len(BATCHES) + 1,)),
             dma((2,)),
             dma((2,)),
             dma((4,)),

time: 51.6 us -> 50.9 us (0.986)
  Pallas kernels: 49.6 us -> 48.8 us
    pallas_call x1, Pallas kernels: 49.6 us -> 48.8 us  [local(): pl.pallas_call(kernel, out_shape=(jax.ShapeDtypeStruct((SHARD, WIDTH), F3...]
where the time goes in v6:
time: 50.9 us; the launch traced here: 50.8 us
  Pallas kernels  48.8 us (96%)
  local copies, waits for them, and re-layouts  1.28 us (3%)
  between operations  0.64 us (1%)
    pallas_call x1, Pallas kernels, local(): pl.pallas_call(kernel, out_shape=(jax.ShapeDtypeStruct((SHARD, WIDTH), F3...  48.8 us
    unnamed x2, local copies, waits for them, and re-layouts  1.28 us

profile of v6, /device:TPU:1, one launch (start us, length us, event | category | flops | bytes accessed | tf_op | source)
XLA Modules:
  0.0 50.8 jit_solution(1595693682693059402)
XLA Ops:
  0.6 48.8 %shard_map.59 = (f32[64,1024]{1,0:T(8,128)S(1)}, f32[512]{0:T(512)S(1)}) custom-call(s32[4,32]{1,0:T(4,128)} %bitcast.2, bf16[512,1024]{1,0:T(8,128)(2,1)} %points_hbm.1, s32[1,512]{1,0:T(1,128)} %bitcast.3, bf16[64,1024]{1,0:T(8,128)(2,1)} %cent_hbm.1), custom_call_target="tpu_custom_call" | custom-call | tf_op jit(solution)/shard_map/pallas_call | solution.py:512
  49.5 0.7 %copy.8 = f32[64,1024]{1,0:T(8,128)} copy(f32[64,1024]{1,0:T(8,128)S(1)} %get-tuple-element.4) | data formatting | bytes 524288
  50.2 0.6 %copy.9 = f32[512]{0:T(512)} copy(f32[512]{0:T(512)S(1)} %get-tuple-element.5) | data formatting | bytes 4096

commit v7 on v6

--- a/solution.py
+++ b/solution.py
@@ -123,6 +123,11 @@
             device_id_type=MESH,
         )
 
+    coarse_in = pltpu.make_async_copy(coarse_hbm, coarse, in_sem.at[0])
+    points_in = pltpu.make_async_copy(points_hbm, points, in_sem.at[1])
+    coarse_in.start()
+    points_in.start()
+
     barrier = pltpu.get_barrier_semaphore()
     for k in range(1, GROUPS):
         pl.semaphore_signal(barrier, inc=1, device_id=(group_at(k), d), device_id_type=MESH)
@@ -136,12 +141,8 @@
                 device_id_type=MESH,
             )
 
-    coarse_in = pltpu.make_async_copy(coarse_hbm, coarse, in_sem.at[0])
-    points_in = pltpu.make_async_copy(points_hbm, points, in_sem.at[1])
     cent_in = pltpu.make_async_copy(cent_hbm, pool.at[d], in_sem.at[2])
     cand_in = pltpu.make_async_copy(cand_hbm, cand, in_sem.at[3])
-    coarse_in.start()
-    points_in.start()
     cent_in.start()
     cand_in.start()
 
@@ -482,16 +483,16 @@
     for k in range(1, 4):
         totals = totals + tot2rx[k]
     column = jnp.sum(jnp.where(diagonal, totals[0:1], 0.0), axis=1, keepdims=True) + PRIOR_WEIGHT
+    scale = 1.0 / column
 
     for axis in (0, 1):
         second = place[axis][1]
-        total = own[axis][second]
+        span = slice(axis * HALF, (axis + 1) * HALF)
+        total = own[axis][second] + PRIOR_WEIGHT * pool[d, :, span].astype(F32)
         arrived(last[axis], last_recv.at[axis])
         for k in range(3):
             total = total + last[axis][k].astype(F32)
-        span = slice(axis * HALF, (axis + 1) * HALF)
-        prior = pool[d, :, span].astype(F32)
-        new_ref[:, span] = (total + PRIOR_WEIGHT * prior) / column
+        new_ref[:, span] = total * scale
 
     left(tx.at[1:GROUPS], row_send)
     left(txf.at[1:GROUPS], flag_sem.at[0])

time: 50.9 us -> 50.7 us (level)
  no operation moved by 1% of the time
where the time goes in v7:
time: 50.7 us; the launch traced here: 50.6 us
  Pallas kernels  48.7 us (96%)
  local copies, waits for them, and re-layouts  1.28 us (3%)
  between operations  0.64 us (1%)
    pallas_call x1, Pallas kernels, local(): pl.pallas_call(kernel, out_shape=(jax.ShapeDtypeStruct((SHARD, WIDTH), F3...  48.7 us
    unnamed x2, local copies, waits for them, and re-layouts  1.28 us

profile of v7, /device:TPU:1, one launch (start us, length us, event | category | flops | bytes accessed | tf_op | source)
XLA Modules:
  0.0 50.6 jit_solution(2865783790212821522)
XLA Ops:
  0.6 48.7 %shard_map.59 = (f32[64,1024]{1,0:T(8,128)S(1)}, f32[512]{0:T(512)S(1)}) custom-call(s32[4,32]{1,0:T(4,128)} %bitcast.2, bf16[512,1024]{1,0:T(8,128)(2,1)} %points_hbm.1, s32[1,512]{1,0:T(1,128)} %bitcast.3, bf16[64,1024]{1,0:T(8,128)(2,1)} %cent_hbm.1), custom_call_target="tpu_custom_call" | custom-call | tf_op jit(solution)/shard_map/pallas_call | solution.py:513
  49.3 0.7 %copy.8 = f32[64,1024]{1,0:T(8,128)} copy(f32[64,1024]{1,0:T(8,128)S(1)} %get-tuple-element.4) | data formatting | bytes 524288
  50.0 0.6 %copy.9 = f32[512]{0:T(512)} copy(f32[512]{0:T(512)S(1)} %get-tuple-element.5) | data formatting | bytes 4096

commit v8 on v7

--- a/solution.py
+++ b/solution.py
@@ -31,7 +31,7 @@
 SUBS = len(SPANS)
 EARLY = 6
 AWAY = ((0, 0), (0, 1), (1, 0), (3, 0), (1, 1), (3, 1), (2, 0), (2, 1))
-ORDER = (2, 3, 4, 5, 6, 7, 1)
+ORDER = ((2, 3), (4, 5), (6, 7), (1, 0))
 BATCHES = ((0, 1), (2, 3), (4, 5), (6,), (7,))
 LAST = GROUPS - 1
 
@@ -163,11 +163,13 @@
         live = (lane_rank[0:1].astype(F32) < held).astype(F32)
         return jnp.broadcast_to(live, (8, SLOTS))
 
-    def pack(owner):
-        here = slot == (slot_ids + owner * SLOTS).astype(F32)
-        return jnp.dot(
-            here.astype(F32).astype(BF16), points[...], preferred_element_type=F32
-        ).astype(BF16)
+    def pack(pair):
+        here = jnp.concatenate(
+            [slot == (slot_ids + group_at(k) * SLOTS).astype(F32) for k in pair], axis=0
+        )
+        rows = jnp.dot(here.astype(F32).astype(BF16), points[...], preferred_element_type=F32)
+        for i, k in enumerate(pair):
+            (tx if k else rx)[k] = rows[i * SLOTS : (i + 1) * SLOTS].astype(BF16)
 
     def columns(axis):
         return pl.ds(axis * HALF, HALF)
@@ -220,32 +222,32 @@
             (g, member(first, turn(second, k2), axis)),
         )
 
-    for k in ORDER:
+    for k in range(1, GROUPS):
         txf[k] = flag(group_at(k))
     rxf[0] = flag(g)
     points_in.wait()
-    tx[ORDER[0]] = pack(group_at(ORDER[0]))
+    pack(ORDER[0])
     pl.semaphore_wait(barrier, GROUPS - 1 + 6)
-    for i, k in enumerate(ORDER):
+    for i, pair in enumerate(ORDER):
         if i:
-            tx[k] = pack(group_at(k))
-        if k == LAST:
-            last_row_copy(0).start()
-            last_row_copy(1).start()
-        else:
-            row_copy(k).start()
-        if i == 1:
-            for k1 in ORDER:
-                flag_copy(k1).start()
+            pack(pair)
+        for k in pair:
+            if k == LAST:
+                last_row_copy(0).start()
+                last_row_copy(1).start()
+            elif k:
+                row_copy(k).start()
+        if i == 0:
+            for k in range(1, GROUPS):
+                flag_copy(k).start()
             cent_in.wait()
             for axis in (0, 1):
                 for k1 in (2, 1, 3):
                     gather1(axis, k1).start()
-        if i == 2:
+        if i == 1:
             for axis in (0, 1):
                 for k2 in (2, 1, 3):
                     gather2(axis, 0, k2).start()
-    rx[0] = pack(g)
 
     for k1 in (1, 3, 2):
         for axis in (0, 1):

time: 50.7 us -> 50.9 us (level)
  no operation moved by 1% of the time
where the time goes in v8:
time: 50.9 us; the launch traced here: 50.7 us
  Pallas kernels  48.8 us (96%)
  local copies, waits for them, and re-layouts  1.28 us (3%)
  between operations  0.64 us (1%)
    pallas_call x1, Pallas kernels, local(): pl.pallas_call(kernel, out_shape=(jax.ShapeDtypeStruct((SHARD, WIDTH), F3...  48.8 us
    unnamed x2, local copies, waits for them, and re-layouts  1.28 us

profile of v8, /device:TPU:1, one launch (start us, length us, event | category | flops | bytes accessed | tf_op | source)
XLA Modules:
  0.0 50.7 jit_solution(18264299482856918643)
XLA Ops:
  0.6 48.8 %shard_map.59 = (f32[64,1024]{1,0:T(8,128)S(1)}, f32[512]{0:T(512)S(1)}) custom-call(s32[4,32]{1,0:T(4,128)} %bitcast.2, bf16[512,1024]{1,0:T(8,128)(2,1)} %points_hbm.1, s32[1,512]{1,0:T(1,128)} %bitcast.3, bf16[64,1024]{1,0:T(8,128)(2,1)} %cent_hbm.1), custom_call_target="tpu_custom_call" | custom-call | tf_op jit(solution)/shard_map/pallas_call | solution.py:515
  49.5 0.7 %copy.8 = f32[64,1024]{1,0:T(8,128)} copy(f32[64,1024]{1,0:T(8,128)S(1)} %get-tuple-element.4) | data formatting | bytes 524288
  50.2 0.6 %copy.9 = f32[512]{0:T(512)} copy(f32[512]{0:T(512)S(1)} %get-tuple-element.5) | data formatting | bytes 4096

commit v9 on v7

--- a/solution.py
+++ b/solution.py
@@ -367,9 +367,9 @@
         target = (g, member(turn(first, step), second, axis))
         if near:
             landing = near_in[axis].at[side, span_of(sub), :, span]
-            return remote(source, landing, part_send.at[axis], near_recv.at[axis, sub], target)
+            return remote(source, landing, part_send, near_recv.at[axis, sub], target)
         landing = far_in[axis].at[side, span_of(sub)]
-        return remote(source, landing, part_send.at[axis], far_recv.at[axis, sub], target)
+        return remote(source, landing, part_send, far_recv.at[axis, sub], target)
 
     def far(axis, sub):
         for side in (0, 1):
@@ -407,7 +407,7 @@
                 remote(
                     send[axis].at[holder],
                     last[axis].at[turn(second, -holder) - 1],
-                    last_send.at[axis],
+                    last_send,
                     last_recv.at[axis],
                     (g, member(first, holder, axis)),
                 ).start()
@@ -455,6 +455,15 @@
         total1(k).start()
     for axis in (0, 1):
         relay(axis, 2)
+    affinity = jnp.zeros((1, ROWS), F32)
+    square_eye = iota((SLOTS, SLOTS), 0) == iota((SLOTS, SLOTS), 1)
+    arrived(affrx.at[1:GROUPS], aff_sem.at[1])
+    for k in range(GROUPS):
+        column = jnp.sum(jnp.where(square_eye, affrx[k, 0:1], 0.0), axis=1, keepdims=True)
+        here = slot == (slot_ids + group_at(k) * SLOTS).astype(F32)
+        affinity = affinity + jnp.sum(jnp.where(here, column, 0.0), axis=0, keepdims=True)
+    aff_ref[...] = affinity.reshape(ROWS)
+
     for axis in (0, 1):
         final(axis, 0)
     arrived(tot1rx.at[1:4], tot_sem.at[1])
@@ -469,15 +478,6 @@
     for axis in (0, 1):
         final(axis, 2)
 
-    affinity = jnp.zeros((1, ROWS), F32)
-    square_eye = iota((SLOTS, SLOTS), 0) == iota((SLOTS, SLOTS), 1)
-    arrived(affrx.at[1:GROUPS], aff_sem.at[1])
-    for k in range(GROUPS):
-        column = jnp.sum(jnp.where(square_eye, affrx[k, 0:1], 0.0), axis=1, keepdims=True)
-        here = slot == (slot_ids + group_at(k) * SLOTS).astype(F32)
-        affinity = affinity + jnp.sum(jnp.where(here, column, 0.0), axis=0, keepdims=True)
-    aff_ref[...] = affinity.reshape(ROWS)
-
     totals = tot2[y]
     arrived(tot2rx.at[1:4], tot_sem.at[3])
     for k in range(1, 4):
@@ -500,9 +500,8 @@
     left(tot1.at[0:3], tot_sem.at[0])
     left(tot2.at[0:3], tot_sem.at[2])
     left(pool.at[0:15], ag_send)
-    for axis in (0, 1):
-        left(part[axis].at[0:3], part_send.at[axis])
-        left(last[axis], last_send.at[axis])
+    left(weights.at[0:12], part_send)
+    left(pool.at[0:3], last_send)
 
 
 def local(points, coarse, candidates, centroids):
@@ -560,10 +559,10 @@
             dma,
             dma((2, 3)),
             dma,
-            dma((2,)),
+            dma,
             dma((2, SUBS)),
             dma((2, SUBS)),
-            dma((2,)),
+            dma,
             dma((2,)),
         ],
         compiler_params=pltpu.CompilerParams(

time: 50.7 us -> 50.7 us (level)
  no operation moved by 1% of the time
where the time goes in v9:
time: 50.7 us; the launch traced here: 50.6 us
  Pallas kernels  48.7 us (96%)
  local copies, waits for them, and re-layouts  1.28 us (3%)
  between operations  0.64 us (1%)
    pallas_call x1, Pallas kernels, local(): pl.pallas_call(kernel, out_shape=(jax.ShapeDtypeStruct((SHARD, WIDTH), F3...  48.7 us
    unnamed x2, local copies, waits for them, and re-layouts  1.28 us

profile of v9, /device:TPU:1, one launch (start us, length us, event | category | flops | bytes accessed | tf_op | source)
XLA Modules:
  0.0 50.6 jit_solution(6099160363191695634)
XLA Ops:
  0.6 48.7 %shard_map.59 = (f32[64,1024]{1,0:T(8,128)S(1)}, f32[512]{0:T(512)S(1)}) custom-call(s32[4,32]{1,0:T(4,128)} %bitcast.2, bf16[512,1024]{1,0:T(8,128)(2,1)} %points_hbm.1, s32[1,512]{1,0:T(1,128)} %bitcast.3, bf16[64,1024]{1,0:T(8,128)(2,1)} %cent_hbm.1), custom_call_target="tpu_custom_call" | custom-call | tf_op jit(solution)/shard_map/pallas_call | solution.py:512
  49.3 0.7 %copy.8 = f32[64,1024]{1,0:T(8,128)} copy(f32[64,1024]{1,0:T(8,128)S(1)} %get-tuple-element.4) | data formatting | bytes 524288
  50.0 0.6 %copy.9 = f32[512]{0:T(512)} copy(f32[512]{0:T(512)S(1)} %get-tuple-element.5) | data formatting | bytes 4096
